TPU v7x, 32 devices: a whole 2x2x4 slice. The times are simulated.
32 devices in a mesh: dp: 16 (over z, y, core), tensor: 2 (over x).
Axes of the slice: x: 2, y: 2, z: 4, core: 2. Of those that a mesh axis runs over, the one named last changes fastest.
Arguments:
- context: bfloat16 [16384, 4096], P(('dp', 'tensor')), may hold values from -6 to 6
- latents: bfloat16 [4096, 4096], P('dp'), may hold values from -6 to 6
- lengths: int32 [16, 4], P('dp'), may hold values from 1 to 768, 1024 in all within a row
- ctx_gain: float32 [4096], replicated, may hold values from 0.25 to 1.75
- lat_gain: float32 [4096], replicated, may hold values from 0.25 to 1.75
- q_weight: bfloat16 [4096, 4096], P('dp', 'tensor'), may hold values from -0.09375 to 0.09375
- key_value_weight: bfloat16 [4096, 1024], P('dp'), may hold values from -0.09375 to 0.09375
- out_weight: bfloat16 [4096, 4096], P('dp', 'tensor'), may hold values from -0.75 to 0.75
- out_grad: bfloat16 [4096, 4096], P(('dp', 'tensor')), may hold values from -6 to 6
Outputs:
- resampled: bfloat16 [4096, 4096], P(('dp', 'tensor'))
- context_grad: float32 [16384, 4096], P(('dp', 'tensor'))
- latents_grad: float32 [4096, 4096], P(('dp', 'tensor'))
- ctx_gain_grad: float32 [4096], P(('dp', 'tensor'))
- lat_gain_grad: float32 [4096], P(('dp', 'tensor'))
- q_weight_grad: float32 [4096, 4096], P('dp', 'tensor')
- kv_weight_grad: float32 [4096, 1024], P(('dp', 'tensor'))
- out_weight_grad: float32 [4096, 4096], P('dp', 'tensor')
Inputs may be any that keep to these rules, and one draw needn't show every extreme that they name: Each row holds 4 positive lengths that sum to 1024; the longest of each row is exactly 768.
All inputs are finite; a program needn't handle non-finite values.
Results may differ from a plain program's by a relative error of at most 0.011.
Values may be sent and summed in bfloat16 or wider, within the bound.
No kernel may reach another device: no remote copies, remote signals or barrier semaphores. Data moves between devices by JAX's collectives and lax.ppermute only.
A program may use at most 320 MiB of HBM per device.

v0:
```python
import math

import jax
import jax.numpy as jnp
from jax import lax
from jax.experimental import pallas as pl
from jax.experimental.pallas import tpu as pltpu
from jax.sharding import PartitionSpec as P

QUERY_HEADS = 32
KEY_VALUE_HEADS = 4
HEAD_SIZE = 128
LAT = 64
IMG_GRP = 4
GROUPED = QUERY_HEADS // KEY_VALUE_HEADS

norm_eps = 1e-06
scale = HEAD_SIZE ** (-0.5)
scale_log2 = scale * math.log2(math.e)
low = jnp.bfloat16
full = jnp.float32
CHUNK = 256
HINT = 1
VMEM_BYTES = 48 * 1024 * 1024


def dot_nt(a, b):
    return lax.dot_general(a, b, (((1,), (1,)), ((), ())), preferred_element_type=full)


def dot_nn(a, b):
    return lax.dot_general(a, b, (((1,), (0,)), ((), ())), preferred_element_type=full)


def stack_heads(wide):
    return jnp.concatenate(
        [wide[:, h * HEAD_SIZE : (h + 1) * HEAD_SIZE] for h in range(GROUPED)], axis=0
    )


def spread_heads(tall):
    return jnp.concatenate([tall[h * LAT : (h + 1) * LAT] for h in range(GROUPED)], axis=1)


def fwd_kernel(bounds, q_ref, kvp_ref, kvl_ref, o_ref, lse_ref, s_scr, m_scr, l_scr, acc_scr):
    image = pl.program_id(0) * IMG_GRP + pl.program_id(1)
    lo = bounds[0, image]
    hi = bounds[1, image]
    chunks = kvp_ref.shape[1] // CHUNK
    qs = stack_heads(q_ref[...])
    s_lat = dot_nt(kvl_ref[:, :HEAD_SIZE], qs) * scale_log2
    m_scr[...] = jnp.max(s_lat, axis=0, keepdims=True)

    @pl.loop(0, chunks)
    def _(j):
        rows = pl.ds(pl.multiple_of(j * CHUNK, CHUNK), CHUNK)

        @pl.when((lo < (j + 1) * CHUNK) & (hi > j * CHUNK))
        def _():
            keys = kvp_ref[0, rows, :HEAD_SIZE]
            s = dot_nt(keys, qs) * scale_log2
            at = lax.broadcasted_iota(jnp.int32, s.shape, 0) + j * CHUNK
            s = jnp.where((at >= lo) & (at < hi), s, -1e30)
            s_scr[rows, :] = s
            m_scr[...] = jnp.maximum(m_scr[...], jnp.max(s, axis=0, keepdims=True))

    top = m_scr[...]
    p = jnp.exp2(s_lat - top)
    l_scr[...] = jnp.sum(p, axis=0, keepdims=True)
    acc_scr[...] = dot_nn(kvl_ref[:, HEAD_SIZE:].T, p.astype(low))

    @pl.loop(0, chunks)
    def _(j):
        rows = pl.ds(pl.multiple_of(j * CHUNK, CHUNK), CHUNK)

        @pl.when((lo < (j + 1) * CHUNK) & (hi > j * CHUNK))
        def _():
            values = kvp_ref[0, rows, HEAD_SIZE:]
            p = jnp.exp2(s_scr[rows, :] - top)
            l_scr[...] += jnp.sum(p, axis=0, keepdims=True)
            acc_scr[...] += dot_nn(values.T, p.astype(low))

    total = l_scr[...]
    lse_ref[0] = top + jnp.log2(total)
    o_ref[...] = spread_heads((acc_scr[...] / total).T).astype(low)


def bwd_kernel(
    bounds, q_ref, do_ref, kvp_ref, kvl_ref, lse_ref,
    dq_ref, dkvp_ref, dkvl_ref,
    p_scr, dp_scr, dkv_scr, dl_scr, dq_scr,
):
    i = pl.program_id(1)
    image = pl.program_id(0) * IMG_GRP + i
    lo = bounds[0, image]
    hi = bounds[1, image]
    chunks = kvp_ref.shape[1] // CHUNK
    qs = stack_heads(q_ref[...])
    dos = stack_heads(do_ref[...])
    lse = lse_ref[0]

    @pl.when(i == 0)
    def _():
        dkv_scr[...] = jnp.zeros_like(dkv_scr)

    k_lat = kvl_ref[:, :HEAD_SIZE]
    p_lat = jnp.exp2(dot_nt(k_lat, qs) * scale_log2 - lse)
    dp_lat = dot_nt(kvl_ref[:, HEAD_SIZE:], dos)
    dl_scr[...] = jnp.sum(p_lat * dp_lat, axis=0, keepdims=True)

    @pl.loop(0, chunks)
    def _(j):
        rows = pl.ds(pl.multiple_of(j * CHUNK, CHUNK), CHUNK)

        @pl.when((lo < (j + 1) * CHUNK) & (hi > j * CHUNK))
        def _():
            s = dot_nt(kvp_ref[0, rows, :HEAD_SIZE], qs) * scale_log2
            at = lax.broadcasted_iota(jnp.int32, s.shape, 0) + j * CHUNK
            s = jnp.where((at >= lo) & (at < hi), s - lse, -1e30)
            p = jnp.exp2(s)
            dp = dot_nt(kvp_ref[0, rows, HEAD_SIZE:], dos)
            dl_scr[...] += jnp.sum(p * dp, axis=0, keepdims=True)
            p_scr[rows, :] = p
            dp_scr[rows, :] = dp

    delta = dl_scr[...]
    ds_lat = (p_lat * (dp_lat - delta) * scale).astype(low)
    dq_scr[...] = dot_nn(k_lat.T, ds_lat)
    dkvl_ref[:, :HEAD_SIZE] = dot_nn(ds_lat, qs).astype(low)
    dkvl_ref[:, HEAD_SIZE:] = dot_nn(p_lat.astype(low), dos).astype(low)

    @pl.loop(0, chunks)
    def _(j):
        rows = pl.ds(pl.multiple_of(j * CHUNK, CHUNK), CHUNK)

        @pl.when((lo < (j + 1) * CHUNK) & (hi > j * CHUNK))
        def _():
            p = p_scr[rows, :]
            ds = (p * (dp_scr[rows, :] - delta) * scale).astype(low)
            dq_scr[...] += dot_nn(kvp_ref[0, rows, :HEAD_SIZE].T, ds)
            dkv_scr[rows, :HEAD_SIZE] += dot_nn(ds, qs)
            dkv_scr[rows, HEAD_SIZE:] += dot_nn(p.astype(low), dos)

    dq_ref[...] = spread_heads(dq_scr[...].T).astype(low)

    @pl.when(i == IMG_GRP - 1)
    def _():
        dkvp_ref[0] = dkv_scr[...].astype(low)


def attention_specs(groups, patches, heads_width):
    rows = pl.BlockSpec((LAT, heads_width), lambda g, i, b: (g * IMG_GRP + i, 0))
    kvp = pl.BlockSpec((1, patches, 2 * HEAD_SIZE), lambda g, i, b: (g, 0, 0))
    kvl = pl.BlockSpec((LAT, 2 * HEAD_SIZE), lambda g, i, b: (g * IMG_GRP + i, 0))
    lse = pl.BlockSpec((1, 1, GROUPED * LAT), lambda g, i, b: (g * IMG_GRP + i, 0, 0))
    return rows, kvp, kvl, lse


def attend(bounds, q, kvp, kvl):
    groups, patches, _ = kvp.shape
    rows, kvp_spec, kvl_spec, lse_spec = attention_specs(groups, patches, q.shape[1])
    wide = GROUPED * LAT
    return pl.pallas_call(
        fwd_kernel,
        grid_spec=pltpu.PrefetchScalarGridSpec(
            num_scalar_prefetch=1,
            grid=(groups, IMG_GRP),
            in_specs=[rows, kvp_spec, kvl_spec],
            out_specs=[rows, lse_spec],
            scratch_shapes=[
                pltpu.VMEM((patches, wide), full),
                pltpu.VMEM((1, wide), full),
                pltpu.VMEM((1, wide), full),
                pltpu.VMEM((HEAD_SIZE, wide), full),
            ],
        ),
        out_shape=[
            jax.ShapeDtypeStruct(q.shape, low),
            jax.ShapeDtypeStruct((groups * IMG_GRP, 1, wide), full),
        ],
        compiler_params=pltpu.CompilerParams(vmem_limit_bytes=VMEM_BYTES),
        cost_estimate=pl.CostEstimate(
            flops=2 * 2 * groups * IMG_GRP * wide * patches * HEAD_SIZE // HINT,
            bytes_accessed=(4 * q.size + 2 * kvp.size) // HINT,
            transcendentals=groups * IMG_GRP * wide * patches // HINT,
        ),
        name="attention_forward",
    )(bounds, q, kvp, kvl)


def attend_back(bounds, q, d_out, kvp, kvl, lse):
    groups, patches, _ = kvp.shape
    rows, kvp_spec, kvl_spec, lse_spec = attention_specs(groups, patches, q.shape[1])
    wide = GROUPED * LAT
    return pl.pallas_call(
        bwd_kernel,
        grid_spec=pltpu.PrefetchScalarGridSpec(
            num_scalar_prefetch=1,
            grid=(groups, IMG_GRP),
            in_specs=[rows, rows, kvp_spec, kvl_spec, lse_spec],
            out_specs=[rows, kvp_spec, kvl_spec],
            scratch_shapes=[
                pltpu.VMEM((patches, wide), full),
                pltpu.VMEM((patches, wide), full),
                pltpu.VMEM((patches, 2 * HEAD_SIZE), full),
                pltpu.VMEM((1, wide), full),
                pltpu.VMEM((HEAD_SIZE, wide), full),
            ],
        ),
        out_shape=[
            jax.ShapeDtypeStruct(q.shape, low),
            jax.ShapeDtypeStruct(kvp.shape, low),
            jax.ShapeDtypeStruct(kvl.shape, low),
        ],
        compiler_params=pltpu.CompilerParams(vmem_limit_bytes=VMEM_BYTES),
        cost_estimate=pl.CostEstimate(
            flops=2 * 5 * groups * IMG_GRP * wide * patches * HEAD_SIZE // 1000,
            bytes_accessed=(6 * q.size + 4 * kvp.size) // 1000,
            transcendentals=groups * IMG_GRP * wide * patches // 1000,
        ),
        name="attention_backward",
    )(bounds, q, d_out, kvp, kvl, lse)


def dot_tn(a, b):
    return lax.dot_general(a, b, (((0,), (0,)), ((), ())), preferred_element_type=full)


def call(kernel, name, scalars, arrays, in_specs, out_specs, out_shape, scratch, grid, flops, hint=1):
    moved = sum(a.size * a.dtype.itemsize for a in arrays)
    moved += sum(o.size * o.dtype.itemsize for o in out_shape)
    return pl.pallas_call(
        kernel,
        grid_spec=pltpu.PrefetchScalarGridSpec(
            num_scalar_prefetch=len(scalars),
            grid=grid,
            in_specs=in_specs,
            out_specs=out_specs,
            scratch_shapes=scratch,
        ),
        out_shape=out_shape,
        compiler_params=pltpu.CompilerParams(vmem_limit_bytes=VMEM_BYTES),
        cost_estimate=pl.CostEstimate(flops=flops // hint, bytes_accessed=moved // hint, transcendentals=0),
        name=name,
    )(*scalars, *arrays)


def whole(shape):
    return pl.BlockSpec(shape, lambda *_: (0,) * len(shape))


def fetch(offsets, pieces, held, sems):
    total = sum(piece.shape[0] for piece in pieces)
    rows = held.shape[0] // offsets.shape[0]
    assert total == held.shape[0]
    copies = []
    for piece in pieces:
        for first in range(0, piece.shape[0], rows):
            n = len(copies)
            at = pl.multiple_of(offsets[n], rows)
            copies.append(
                pltpu.make_async_copy(
                    piece.at[pl.ds(first, rows)], held.at[pl.ds(at, rows)], sems.at[n]
                )
            )
    for copy in copies:
        copy.start()
    for copy in copies:
        copy.wait()


def rows_kernel(count, offsets, act, *refs):
    pieces, (out, held, sems) = refs[:count], refs[count:]
    fetch(offsets, pieces, held, sems)
    step = 512

    @pl.loop(0, out.shape[1] // step)
    def _(n):
        span = pl.ds(pl.multiple_of(n * step, step), step)
        out[:, span] = dot_nn(act[...], held[:, span]).astype(out.dtype)


def rows_times_weight(act, weight):
    offsets, pieces = weight
    cols = pieces[0].shape[1]
    rows, features = act.shape
    return call(
        lambda *refs: rows_kernel(len(pieces), *refs),
        "rows_times_weight",
        [offsets],
        [act, *pieces],
        [whole(act.shape)] + [pl.BlockSpec(memory_space=pltpu.HBM)] * len(pieces),
        [whole((rows, cols))],
        [jax.ShapeDtypeStruct((rows, cols), low)],
        [pltpu.VMEM((features, cols), low), pltpu.SemaphoreType.DMA((offsets.shape[0],))],
        (1,),
        2 * rows * features * cols,
    )[0]


def rows_times_kv(act, weight):
    offsets, pieces = weight
    rows, features = act.shape
    cols = pieces[0].shape[1]
    count = len(pieces)

    def kernel(offsets_ref, act_ref, *refs):
        out, held, sems = refs[count:]
        fetch(offsets_ref, refs[:count], held, sems)
        step = 512

        @pl.loop(0, cols // step)
        def _(n):
            span = pl.ds(pl.multiple_of(n * step, step), step)
            out[:, span] = dot_nn(act_ref[...], held[:, span]).astype(low)

    return call(
        kernel,
        "rows_times_kv",
        [offsets],
        [act, *pieces],
        [whole(act.shape)] + [pl.BlockSpec(memory_space=pltpu.HBM)] * count,
        [whole((rows, cols)), whole((features, cols))],
        [jax.ShapeDtypeStruct((rows, cols), low), jax.ShapeDtypeStruct((features, cols), low)],
        [pltpu.SemaphoreType.DMA((offsets.shape[0],))],
        (1,),
        2 * rows * features * cols,
    )


def split_features(features, part):
    first = features * part // 8
    return [first, first, features - first, features - first]


def keep_and_send(x, outs, held, step, value_of):
    a_keep, a_sent, b_keep, b_sent = outs
    rows, first = a_keep.shape[1], a_keep.shape[2]

    def parts_of(n, start):
        value = value_of(pl.ds(pl.multiple_of(start + n * step, step), step))
        return [value[k * rows : (k + 1) * rows] for k in range(4)]

    @pl.loop(0, first // step)
    def _(n):
        parts = parts_of(n, 0)
        span = pl.ds(pl.multiple_of(n * step, step), step)
        for k in range(2):
            a_keep[k, :, span] = parts[k]
            a_sent[k, :, span] = parts[2 + k]

    @pl.loop(0, (held.shape[0] - first) // step)
    def _(n):
        parts = parts_of(n, first)
        span = pl.ds(pl.multiple_of(n * step, step), step)
        for g in range(2):
            b_keep[g, :, span] = jnp.where(x == 0, parts[2 * g], parts[2 * g + 1])
            b_sent[g, :, span] = jnp.where(x == 0, parts[2 * g + 1], parts[2 * g])


def heads_kernel(count, offsets, place, act, *refs):
    pieces, outs, (held, sems) = refs[:count], refs[count:-2], refs[-2:]
    fetch(offsets, pieces, held, sems)
    keep_and_send(
        place[0], outs, held, 512, lambda span: dot_nt(act[...], held[span, :]).astype(low)
    )


def heads_times_weight(place, act, weight):
    offsets, pieces = weight
    rows, cols = act.shape
    features = sum(piece.shape[0] for piece in pieces)
    halves = [(2, rows // 4, n) for n in split_features(features, 3)]
    return call(
        lambda *refs: heads_kernel(len(pieces), *refs),
        "heads_times_weight",
        [offsets, place],
        [act, *pieces],
        [whole(act.shape)] + [pl.BlockSpec(memory_space=pltpu.HBM)] * len(pieces),
        [whole(half) for half in halves],
        [jax.ShapeDtypeStruct(half, low) for half in halves],
        [pltpu.VMEM((features, cols), low), pltpu.SemaphoreType.DMA((offsets.shape[0],))],
        (1,),
        2 * rows * features * cols,
        hint=1000,
    )


def lat_back_kernel(count, offsets, place, act, kv_act, kv, lat_a, lat_b, scales, *refs):
    pieces, outs, (gain, held, sems) = refs[:count], refs[count:-3], refs[-3:]
    fetch(offsets, pieces, held, sems)

    def value_of(span):
        value = dot_nt(act[...], held[span, :]) + dot_nt(kv_act[...], kv[span, :])
        lat = jnp.concatenate([lat_a[:, span], lat_b[:, span]], axis=0)
        unit = lat.astype(full) * scales[:, :1]
        gain[:, span] = jnp.sum(value * unit, axis=0, keepdims=True)
        return value.astype(low)

    keep_and_send(place[0], outs, held, 512, value_of)


def lat_back(place, d_queries, weight, d_kv, kv, lat_a, lat_b, scales):
    offsets, pieces = weight
    rows, cols = d_queries.shape
    features = sum(piece.shape[0] for piece in pieces)
    halves = [(2, rows // 4, n) for n in split_features(features, 4)]
    arrays = [d_queries, d_kv, kv, lat_a, lat_b, scales]
    *parts, gain = call(
        lambda *refs: lat_back_kernel(len(pieces), *refs),
        "lat_back",
        [offsets, place],
        [*arrays, *pieces],
        [whole(a.shape) for a in arrays] + [pl.BlockSpec(memory_space=pltpu.HBM)] * len(pieces),
        [whole(half) for half in halves] + [whole((1, features))],
        [jax.ShapeDtypeStruct(half, low) for half in halves] + [jax.ShapeDtypeStruct((1, features), full)],
        [pltpu.VMEM((features, cols), low), pltpu.SemaphoreType.DMA((offsets.shape[0],))],
        (1,),
        2 * rows * features * (cols + kv.shape[1]),
    )
    return parts, gain


BLOCK = 256


def weight_grad(act, heads, blocks):
    rows, cols = heads.shape
    count = blocks.shape[0]

    def kernel(at, act_ref, heads_ref, out):
        out[0] = dot_tn(act_ref[...], heads_ref[...]).astype(low)

    return call(
        kernel,
        "weight_grad",
        [blocks],
        [act, heads],
        [pl.BlockSpec((rows, BLOCK), lambda i, at: (0, at[i])), whole(heads.shape)],
        [pl.BlockSpec((1, BLOCK, cols), lambda i, at: (i, 0, 0))],
        [jax.ShapeDtypeStruct((count, BLOCK, cols), low)],
        [],
        (count,),
        2 * rows * count * BLOCK * cols,
    )[0]


def kv_weight_grad_part(place, ctx_n, d_kv, lat_n, d_kv_lat, blocks):
    rows, cols = d_kv.shape
    count = blocks.shape[0]

    def kernel(at, here, ctx_ref, d_kv_ref, lat_ref, d_lat_ref, out, total):
        total[...] = dot_tn(ctx_ref[...], d_kv_ref[...])
        lat_part = dot_tn(lat_ref[...], d_lat_ref[...])
        first = here[0] * (cols // 2) + here[1] * HEAD_SIZE
        for k in range(2):
            at_k = pl.multiple_of(first + k * (cols // 4), HEAD_SIZE)
            span = pl.ds(at_k, HEAD_SIZE)
            total[:, span] += lat_part[:, k * HEAD_SIZE : (k + 1) * HEAD_SIZE]
        half = total.shape[0] // 2
        for k in range(2):
            at_x = pl.multiple_of((here[0] ^ k) * half, half)
            out[k, 0] = total[pl.ds(at_x, half), :].astype(low)

    block = pl.BlockSpec((rows, BLOCK), lambda i, at, here: (0, at[i]))
    return call(
        kernel,
        "kv_weight_grad",
        [blocks, place],
        [ctx_n, d_kv, lat_n, d_kv_lat],
        [block, whole(d_kv.shape), block, whole(d_kv_lat.shape)],
        [pl.BlockSpec((2, 1, BLOCK // 2, cols), lambda i, at, here: (0, i, 0, 0))],
        [jax.ShapeDtypeStruct((2, count, BLOCK // 2, cols), low)],
        [pltpu.VMEM((BLOCK, cols), full)],
        (count,),
        2 * rows * count * BLOCK * (cols + 2 * HEAD_SIZE),
    )[0]


NORM_ROWS = 64


def norm_rows(sources, gain):
    rows, features = sources[0].shape
    steps = rows // NORM_ROWS
    count = len(sources)

    def kernel(*refs):
        gain_ref, out, scale_out = refs[count:]
        for n in range(count):

            @pl.when(pl.program_id(0) == n)
            def _():
                values = refs[n][...].astype(full)
                scale_rows = lax.rsqrt(jnp.mean(values * values, axis=1, keepdims=True) + norm_eps)
                out[...] = (values * scale_rows * gain_ref[...]).astype(low)
                scale_out[...] = jnp.broadcast_to(scale_rows, scale_out.shape)

    def source_spec(n):
        return pl.BlockSpec(
            (NORM_ROWS, features), lambda s, i: (jnp.where(s == n, i, 0), 0)
        )

    return call(
        kernel,
        "norm_rows",
        [],
        [*sources, gain[None]],
        [source_spec(n) for n in range(count)] + [whole((1, features))],
        [
            pl.BlockSpec((NORM_ROWS, features), lambda s, i: (s * steps + i, 0)),
            pl.BlockSpec((NORM_ROWS, 128), lambda s, i: (s * steps + i, 0)),
        ],
        [
            jax.ShapeDtypeStruct((count * rows, features), low),
            jax.ShapeDtypeStruct((count * rows, 128), full),
        ],
        [],
        (count, steps),
        4 * count * rows * features,
        hint=1,
    )


def ctx_back(d_kv, full_kv, context, scales, gain):
    rows, cols = d_kv.shape
    features = full_kv.shape[0]
    step = 128

    def kernel(d_ref, kv_ref, ctx_ref, scale_ref, gain_ref, out, gain_out):
        @pl.when(pl.program_id(0) == 0)
        def _():
            gain_out[...] = jnp.zeros_like(gain_out)

        d = dot_nt(d_ref[...], kv_ref[...])
        scale_rows = scale_ref[:, :1]
        unit = ctx_ref[...].astype(full) * scale_rows
        weighted = d * unit
        gain_out[...] += jnp.sum(weighted, axis=0, keepdims=True)
        inner = jnp.mean(weighted * gain_ref[...], axis=1, keepdims=True)
        out[...] = scale_rows * (d * gain_ref[...] - unit * inner)

    return call(
        kernel,
        "ctx_back",
        [],
        [d_kv, full_kv, context, scales, gain[None]],
        [
            pl.BlockSpec((step, cols), lambda i: (i, 0)),
            whole(full_kv.shape),
            pl.BlockSpec((step, features), lambda i: (i, 0)),
            pl.BlockSpec((step, 128), lambda i: (i, 0)),
            whole((1, features)),
        ],
        [pl.BlockSpec((step, features), lambda i: (i, 0)), whole((1, features))],
        [jax.ShapeDtypeStruct((rows, features), full), jax.ShapeDtypeStruct((1, features), full)],
        [],
        (rows // step,),
        2 * rows * cols * features,
        hint=1,
    )


def after(value, *earlier):
    if not earlier:
        return value
    return lax.optimization_barrier((value, *earlier))[0]


class Place:
    def __init__(self):
        dp = lax.axis_size("dp")
        me = lax.axis_index("dp")
        self.dp = dp
        self.depth = dp // 4
        self.z = me // 4
        self.y = (me // 2) % 2
        self.c = me % 2
        self.x = lax.axis_index("tensor")
        self.scalars = jnp.stack([self.x, self.y]).astype(jnp.int32)
        self.perm_core = [(i, i ^ 1) for i in range(dp)]
        self.perm_y = [(i, i ^ 2) for i in range(dp)]
        self.perm_ring = [(i, (i + 4) % dp) for i in range(dp)]
        self.y_groups = [[i for i in range(dp) if (i // 2) % 2 == y] for y in range(2)]
        self.z_groups = [list(range(k, dp, 4)) for k in range(4)]
        self.manual = self.depth == 4

    def over_core(self, v):
        return lax.ppermute(v, "dp", self.perm_core)

    def over_y(self, v):
        return lax.ppermute(v, "dp", self.perm_y)

    def over_x(self, v):
        return lax.ppermute(v, "tensor", [(0, 1), (1, 0)])

    def ring(self, v, *earlier):
        return lax.ppermute(after(v, *earlier), "dp", self.perm_ring)

    def shift(self, v, r):
        return lax.ppermute(v, "dp", [(i, (i + 4 * r) % self.dp) for i in range(self.dp)])

    def row_blocks(self):
        return [
            (z * 2 + (self.y ^ y_other)) * 2 + c
            for z in range(self.depth)
            for c in range(2)
            for y_other in range(2)
        ]

    def block(self, r, y_other, c_other):
        z = (self.z - r) % self.depth
        return (z * 2 + (self.y ^ y_other)) * 2 + (self.c ^ c_other)


def ordered(at, mine, other, axis):
    first = jnp.where(at == 0, mine, other)
    second = jnp.where(at == 0, other, mine)
    return jnp.concatenate([first, second], axis=axis)


def pick(v, at, axis):
    return lax.dynamic_index_in_dim(v, at, axis, keepdims=False)


def add(a, b):
    return a.astype(full) + b.astype(full)


def group_cols(v, x):
    half = v.shape[1] // 2
    return lax.dynamic_slice_in_dim(v, x * half, half, 1)


def head_cols(v, y):
    keys = lax.dynamic_slice_in_dim(v, y * HEAD_SIZE, HEAD_SIZE, 1)
    values = lax.dynamic_slice_in_dim(v, (2 + y) * HEAD_SIZE, HEAD_SIZE, 1)
    return jnp.concatenate([keys, values], axis=1)


def join_heads(y, mine, other):
    first = jnp.where(y == 0, mine, other)
    second = jnp.where(y == 0, other, mine)
    return jnp.concatenate(
        [
            first[:, :HEAD_SIZE],
            second[:, :HEAD_SIZE],
            first[:, HEAD_SIZE:],
            second[:, HEAD_SIZE:],
        ],
        axis=1,
    )


class WeightBlock:
    def __init__(self, here, weight):
        self.here = here
        self.rows, cols = weight.shape
        half = cols // 2
        if not here.manual:
            held = lax.all_gather(weight, "dp", axis=0, tiled=True)
            self.from_y = lax.dynamic_slice_in_dim(held, here.y * half, half, 1)
            return
        mine = lax.dynamic_slice_in_dim(weight, here.y * half, half, 1)
        sent = lax.dynamic_slice_in_dim(weight, (1 - here.y) * half, half, 1)
        self.from_y = here.over_y(sent)
        self.block = jnp.concatenate([mine, self.from_y], axis=0)

    def result(self, *wait):
        here = self.here
        if not here.manual:
            return jnp.zeros((1,), jnp.int32), [self.from_y]
        held = lax.all_gather(
            after(self.block, *wait), "dp", axis=0, tiled=True, axis_index_groups=here.y_groups
        )
        offsets = [row * self.rows for row in here.row_blocks()]
        return jnp.stack(offsets).astype(jnp.int32), [held]


class GatherKv:
    def __init__(self, here, weight):
        self.here = here
        self.rows = weight.shape[0] // 2
        if here.manual:
            mine = lax.dynamic_slice_in_dim(weight, here.x * self.rows, self.rows, 0)
            self.first = [here.shift(mine, r) for r in (1, 3, 2)]
            self.held = jnp.concatenate([mine] + [self.first[k] for k in (0, 2, 1)], axis=0)
        else:
            self.held = lax.all_gather(weight, "dp", axis=0, tiled=True)
            self.first = [self.held]

    def over_y(self, *wait):
        if self.here.manual:
            from_y = self.here.over_y(after(self.held, *wait))
            self.near = jnp.concatenate([self.held, from_y], axis=0)
            return from_y
        return self.held

    def over_x(self, *wait):
        if self.here.manual:
            self.far = self.here.over_x(after(self.near, *wait))
            return self.far
        return self.held

    def result(self, *wait):
        here = self.here
        if not here.manual:
            return jnp.zeros((1,), jnp.int32), [self.held]
        pieces = [self.near, self.far]
        pieces += [here.over_core(self.near), here.over_core(after(self.far, *wait))]
        offsets = [
            here.block(r, y, c) * 2 * self.rows + (here.x ^ x) * self.rows
            for c in range(2)
            for x in range(2)
            for y in range(2)
            for r in range(4)
        ]
        return jnp.stack(offsets).astype(jnp.int32), pieces


def scatter_rows_of_y(here, act, heads):
    cols = heads.shape[1]
    features = act.shape[1]
    if here.manual:
        blocks = here.row_blocks()[::2]
        part = weight_grad(act, heads, jnp.stack(blocks).astype(jnp.int32))
    else:
        part = weight_grad(act, heads, jnp.arange(features // BLOCK, dtype=jnp.int32))
        part = pick(part.reshape(here.depth, 2, 2, -1, cols), here.y, 1)
    part = part.reshape(features // 2, cols)
    total = lax.psum_scatter(
        part, "dp", scatter_dimension=0, tiled=True, axis_index_groups=here.y_groups
    )
    return part, total.astype(full)


def scatter_weight(here, act, heads):
    cols = heads.shape[1]
    features = act.shape[1]
    if here.manual:
        part = weight_grad(act, heads, jnp.stack(here.row_blocks()).astype(jnp.int32))
    else:
        part = weight_grad(act, heads, jnp.arange(features // BLOCK, dtype=jnp.int32))
        part = part.reshape(here.depth, 2, 2, -1, cols)
        part = jnp.stack([pick(part, here.y, 1), pick(part, 1 - here.y, 1)], axis=2)
    part = part.reshape(features, cols)
    total = lax.psum_scatter(
        part, "dp", scatter_dimension=0, tiled=True, axis_index_groups=here.y_groups
    )

    def result(*wait):
        own, other = jnp.split(after(total, *wait), 2, axis=0)
        from_y = here.over_y(other)
        return ordered(here.y, own.astype(full), from_y.astype(full), 1), from_y

    return part, result


class ScatterKv:
    def __init__(self, here, ctx_n, d_kv, lat_n, d_kv_lat):
        self.here = here
        self.cols = d_kv.shape[1]
        self.args = (ctx_n, d_kv, lat_n, d_kv_lat)
        if not here.manual:
            every = jnp.arange(ctx_n.shape[1] // BLOCK, dtype=jnp.int32)
            part = kv_weight_grad_part(here.scalars, *self.args, every)
            part = ordered(here.x, part[0][:, None], part[1][:, None], 1)
            self.other_part = part.reshape(-1, self.cols)
            return
        self.other_part = self.part(d_kv, 1)
        self.received = here.over_core(self.other_part)

    def part(self, d_kv, c_other):
        here = self.here
        ctx_n, _, lat_n, d_kv_lat = self.args
        blocks = [here.block(r, y, c_other) for y in range(2) for r in range(here.depth)]
        blocks = jnp.stack(blocks).astype(jnp.int32)
        part = kv_weight_grad_part(here.scalars, ctx_n, d_kv, lat_n, d_kv_lat, blocks)
        return part.reshape(2, 2, here.depth, BLOCK // 2, self.cols)

    def own(self, *wait):
        self.own_part = self.other_part
        if self.here.manual:
            self.own_part = self.part(after(self.args[1], self.other_part, *wait), 0)

    def start(self, *wait):
        here = self.here
        if not here.manual:
            self.sent = self.first = self.last = [self.other_part]
            total = lax.psum_scatter(
                self.other_part, ("dp", "tensor"), scatter_dimension=0, tiled=True
            )
            self.total = total.astype(full)
            return
        mine, received = self.own_part, self.received
        half = self.cols // 2
        self.sent = [
            add(mine[:, 1, ..., :half], received[:, 1, ..., :half]).astype(low),
            add(mine[1, ..., half:], received[1, ..., half:]).astype(low),
        ]
        self.first = [
            here.over_y(after(self.sent[0], *wait)),
            here.over_x(after(self.sent[1], *wait)),
        ]
        self.halves = [
            add(mine[:, 0, ..., :half], received[:, 0, ..., :half]) + self.first[0],
            add(mine[0, ..., half:], received[0, ..., half:]) + self.first[1],
        ]

    def go_on(self, *wait):
        here = self.here
        if not here.manual:
            return
        a, b = self.halves
        self.last = [
            here.over_x(after(a[1].astype(low), *wait)),
            here.over_y(after(b[1].astype(low), *wait)),
        ]
        a, b = a[0] + self.last[0], b[0] + self.last[1]
        self.total = jnp.concatenate([a, b], axis=-1)

    def result(self, wait, *late):
        here, total = self.here, self.total
        if not here.manual:
            self.over_z = [total]
            return total
        held = [here.shift(after(total[r].astype(low), *wait), -r) for r in (1, 2, 3)]
        self.over_z = held
        return after(total[0], *late) + held[0] + held[1] + held[2]


class ScatterRows:
    def __init__(self, here, a_keep, a_sent, b_keep, b_sent, y_wait=(), x_wait=()):
        self.here = here
        self.keep = [a_keep, b_keep]
        self.first = [here.over_y(after(a_sent, *y_wait)), here.over_x(after(b_sent, *x_wait))]

    def prepare(self, *wait):
        here = self.here
        (a_keep, b_keep), (a, b) = self.keep, [after(v, *wait) for v in self.first]
        self.sent = [
            add(pick(a_keep, 1 - here.x, 0), pick(a, 1 - here.x, 0)).astype(low),
            add(b_keep[1], b[1]).astype(low),
        ]

    def finish(self, x_wait=(), y_wait=()):
        here = self.here
        self.last = [
            here.over_x(after(self.sent[0], *x_wait)),
            here.over_y(after(self.sent[1], *y_wait)),
        ]

    def result(self, *wait):
        here = self.here
        (a_keep, b_keep), (a, b) = self.keep, self.first
        a_last, b_last = [after(v, *wait) for v in self.last]
        a = add(pick(a_keep, here.x, 0), pick(a, here.x, 0)) + a_last
        b = add(b_keep[0], b[0]) + b_last
        return jnp.concatenate([a, b], axis=-1)


def gather_gains(here, part):
    if not here.manual:
        return part
    part = part.reshape(2, here.depth, 2, 2, 2, -1)
    part = pick(part, here.c, 3) + here.over_core(pick(part, 1 - here.c, 3))
    mine = [pick(part, (here.z - r) % here.depth, 1) for r in range(4)]
    return mine[0] + here.shift(mine[1], -1) + here.shift(mine[2], -2) + here.shift(mine[3], -3)


def scatter_gains(here, part):
    if not here.manual:
        devices = here.dp * 2
        part = part.reshape(2, devices, -1).swapaxes(0, 1)
        return lax.psum_scatter(part, ("dp", "tensor"), scatter_dimension=0)
    part = pick(part, here.x, 2) + here.over_x(pick(part, 1 - here.x, 2))
    return pick(part, here.y, 1) + here.over_y(pick(part, 1 - here.y, 1))


def norm_back(grad_rows, values, gain):
    scale_rows = lax.rsqrt(jnp.mean(values * values, axis=-1, keepdims=True) + norm_eps)
    unit_rows = values * scale_rows
    grad_unit = grad_rows * gain
    inner = jnp.mean(grad_unit * unit_rows, axis=-1, keepdims=True)
    return scale_rows * (grad_unit - unit_rows * inner)


def per_device(
    context, latents, lengths, ctx_gain, lat_gain, q_weight, key_value_weight, out_weight, out_grad
):
    here = Place()
    group_rows = latents.shape[0]
    my_rows = group_rows // 2
    features = context.shape[1]
    patch_rows = context.shape[0]

    kv = GatherKv(here, key_value_weight)
    lengths_y = here.over_y(lengths)
    q_block = WeightBlock(here, q_weight)
    out_block = WeightBlock(here, out_weight)
    full_q = q_block.result(*kv.first, lengths_y, out_block.from_y)
    first = [q_block.from_y, out_block.from_y, *kv.first]
    kv_from_y = kv.over_y(*first)
    grad_x = here.over_x(after(out_grad, *first))
    ctx_n, ctx_scales = norm_rows([after(context, *first)], ctx_gain)
    second = [kv_from_y, grad_x, ctx_n]
    kv_from_x = kv.over_x(*second)
    lat_other = here.over_y(after(latents, *second))
    full_kv = kv.result(lat_other)
    full_out = out_block.result(full_q[1][0], *full_kv[1][-2:], lat_other)
    both_lengths = jnp.concatenate([lengths, lengths_y], axis=0)
    ends = jnp.cumsum(both_lengths, axis=1)
    bounds = jnp.stack([(ends - both_lengths).reshape(-1), ends.reshape(-1)])

    kv_mine, kv_weight = rows_times_kv(ctx_n, full_kv)
    own_kv = head_cols(group_cols(kv_weight, here.x), here.y)
    kv_x = here.over_x(group_cols(kv_mine, 1 - here.x))
    grad_y_a = here.over_y(after(grad_x, lat_other, kv_from_x))
    lat_n, lat_scales = norm_rows([latents, after(lat_other, kv_mine, grad_y_a)], lat_gain)
    by_x = ordered(here.x, group_cols(kv_mine, here.x), kv_x, 0)
    kv_y = here.over_y(after(head_cols(by_x, 1 - here.y), lat_n, full_q[1][0]))
    kv_patch = jnp.stack([head_cols(by_x, here.y), kv_y])
    grad_y_b = here.over_y(after(out_grad, kv_y))

    kv_latent = jnp.dot(lat_n, own_kv, preferred_element_type=full).astype(low)
    queries = rows_times_weight(lat_n, full_q)

    mixed, lse = attend(bounds, queries, kv_patch, kv_latent)
    grad_all = jnp.stack([out_grad, grad_x, after(grad_y_b, mixed), after(grad_y_a, mixed)])
    grad_all = grad_all.reshape(2, 2, my_rows, features)
    grad_all = ordered(here.x, grad_all[:, :1], grad_all[:, 1:], 1)
    grad_all = grad_all.reshape(2 * group_rows, features)
    out_part, out_result = scatter_weight(here, grad_all, mixed)
    d_mixed = rows_times_weight(after(grad_all, out_part), full_out)
    d_queries, d_kv_patch, d_kv_latent = attend_back(
        bounds, queries, d_mixed, kv_patch, kv_latent, lse
    )
    d_group_y = here.over_y(d_kv_patch[1])
    branch_parts = heads_times_weight(here.scalars, after(mixed, d_queries), full_out)
    d_group = join_heads(here.y, d_kv_patch[0], d_group_y).reshape(2, patch_rows, -1)

    d_group_x = here.over_x(after(pick(d_group, 1 - here.x, 0), branch_parts[0]))
    d_kv_mine = ordered(here.x, pick(d_group, here.x, 0), d_group_x, 1)
    d_queries_y = here.over_y(after(d_queries, d_group_y, branch_parts[0]))
    lat_parts, lat_gain_part = lat_back(
        here.scalars, after(d_queries, d_group_y), full_q, d_kv_latent, own_kv,
        latents, lat_other, lat_scales,
    )
    kv_sum = ScatterKv(here, ctx_n, after(d_kv_mine, lat_parts[0]), lat_n, d_kv_latent)
    d_queries_y = jnp.concatenate([d_queries_y[group_rows:], d_queries_y[:group_rows]], axis=0)
    d_queries_all = ordered(here.y, d_queries, d_queries_y, 1)
    kv_sum.own()
    branch = ScatterRows(here, *branch_parts, [d_group_y], [d_group_y])
    q_part, q_weight_grad = scatter_rows_of_y(
        here, after(lat_n, kv_sum.own_part, *branch.first), d_queries_all
    )
    kv_sum.start()
    branch.prepare(*kv_sum.sent)
    branch.finish()
    context_grad, ctx_gain_part = ctx_back(
        after(d_kv_mine, *kv_sum.sent), kv_weight, context, ctx_scales, ctx_gain
    )
    gains = jnp.concatenate([after(ctx_gain_part, *kv_sum.first), lat_gain_part], axis=0)
    gains = gather_gains(here, gains)

    second = [*kv_sum.first, *branch.last, ctx_gain_part]
    lat_sum = ScatterRows(here, *lat_parts, second, second)
    kv_sum.go_on(*second)
    third = [*kv_sum.last, *lat_sum.first]
    kv_weight_grad = kv_sum.result(third, q_weight_grad)
    lat_sum.prepare()
    lat_sum.finish(third, third)
    out_weight_grad, _ = out_result(*third)
    gains = scatter_gains(here, after(gains, *third))
    lat_mine = lax.dynamic_slice_in_dim(latents, here.x * my_rows, my_rows, 0).astype(full)
    resampled = (lat_mine + branch.result()).astype(low)
    latents_grad = out_grad.astype(full) + norm_back(lat_sum.result(), lat_mine, lat_gain)
    return (
        resampled,
        context_grad,
        latents_grad,
        gains[0],
        gains[1],
        q_weight_grad,
        kv_weight_grad,
        out_weight_grad,
    )


def solution(mesh):
    in_specs = (
        P(("dp", "tensor"), None),
        P("dp", None),
        P("dp", None),
        P(),
        P(),
        P("dp", "tensor"),
        P("dp", None),
        P("dp", "tensor"),
        P(("dp", "tensor"), None),
    )
    out_specs = (
        P(("dp", "tensor"), None),
        P(("dp", "tensor"), None),
        P(("dp", "tensor"), None),
        P(("dp", "tensor")),
        P(("dp", "tensor")),
        P("dp", "tensor"),
        P(("dp", "tensor"), None),
        P("dp", "tensor"),
    )
    return jax.shard_map(
        per_device, mesh=mesh, in_specs=in_specs, out_specs=out_specs, check_vma=False
    )
```

profile of v0, /device:TPU:0, one launch (start us, length us, event | category | flops | bytes accessed | tf_op | source)
XLA Modules:
  0.0 440.3 jit_solution(16978245861027045899)
XLA Ops:
  7.3 2.1 constant_dynamic-slice_fusion.14
  9.4 3.0 collective-permute-start.4
  13.4 1.7 constant_dynamic-update-slice_fusion.4
  15.1 4.1 collective-permute-start.3
  20.3 5.1 %collective-permute-done.4 = bf16[256,1024]{1,0:T(8,128)(2,1)S(1)} collective-permute-done((bf16[256,1024]{1,0:T(8,128)(2,1)}, bf16[256,1024]{1,0:T(8,128)(2,1)S(1)}, u32[]{:S(2)}, u32[]{:S(2)}) %collective-permute-start.4) | collective-permute-done | bytes 524320 | tf_op jit(solution)/shard_map/ppermute | solution.py:592
  25.3 2.1 collective-permute-start
  28.4 7.4 %collective-permute-done = s32[1,4]{1,0:T(1,128)S(1)} collective-permute-done((s32[1,4]{1,0:T(1,128)S(1)}, s32[1,4]{1,0:T(1,128)S(1)}, u32[]{:S(2)}, u32[]{:S(2)}) %collective-permute-start) | collective-permute-done | bytes 48 | tf_op jit(solution)/shard_map/ppermute | solution.py:592
  35.9 5.5 %collective-permute-done.2 = bf16[128,1024]{1,0:T(8,128)(2,1)} collective-permute-done((bf16[128,1024]{1,0:T(8,128)(2,1)}, bf16[128,1024]{1,0:T(8,128)(2,1)}, u32[]{:S(2)}, u32[]{:S(2)}) %collective-permute-start.2) | collective-permute-done | bytes 262176 | tf_op jit(solution)/shard_map/ppermute | solution.py:601
  50.0 5.8 %norm_rows.2 = (bf16[512,4096]{1,0:T(8,128)(2,1)S(1)}, f32[512,128]{1,0:T(8,128)S(1)}) custom-call(bf16[512,4096]{1,0:T(8,128)(2,1)} %ctx_ref.1, f32[1,4096]{1,0:T(1,128)S(1)} %bitcast.195), custom_call_target="tpu_custom_call" | custom-call | flops 8388608 | bytes 8667136 | tf_op jit(solution)/shard_map/norm_rows/pallas_call | solution.py:232
  55.9 1.9 copy-done.1
  57.8 8.3 %collective-permute-done.6 = bf16[512,1024]{1,0:T(8,128)(2,1)S(1)} collective-permute-done((bf16[512,1024]{1,0:T(8,128)(2,1)S(1)}, bf16[512,1024]{1,0:T(8,128)(2,1)S(1)}, u32[]{:S(2)}, u32[]{:S(2)}) %collective-permute-start.6) | collective-permute-done | bytes 1048608 | tf_op jit(solution)/shard_map/ppermute | solution.py:592
  70.3 42.1 %collective-permute-done.8.refs_1_.refs_6_ = bf16[256,4096]{1,0:T(8,128)(2,1)S(1)} collective-permute-done((bf16[256,4096]{1,0:T(8,128)(2,1)S(1)}, bf16[256,4096]{1,0:T(8,128)(2,1)S(1)}, u32[]{:S(2)}, u32[]{:S(2)}) %collective-permute-start.8) | collective-permute-done | bytes 2097184 | tf_op jit(solution)/shard_map/ppermute | solution.py:592
  113.9 2.1 pad_maximum_fusion.9
  116.0 2.4 collective-permute-done.11.refs_3_
  118.4 5.6 %all-gather.3.cloned.1.call-done.refs_2_.refs_8_ = bf16[4096,1024]{1,0:T(8,128)(2,1)} async-done(((bf16[512,1024]{1,0:T(8,128)(2,1)}), bf16[4096,1024]{1,0:T(8,128)(2,1)}) %all-gather.3.cloned.1.call-update) | async-done | bytes 8388624 | tf_op jit(solution)/shard_map/all_gather | solution.py:673
  127.6 12.2 %rows_times_kv.1 = (bf16[512,1024]{1,0:T(8,128)(2,1)S(1)}, bf16[4096,1024]{1,0:T(8,128)(2,1)}) custom-call(s32[32]{0:T(128)S(1)} %stack.372.offsets_ref, bf16[512,4096]{1,0:T(8,128)(2,1)} %copy-done.1, bf16[1024,1024]{1,0:T(8,128)(2,1)S(1)} %copy-done.29, bf16[1024,1024]{1,0:T(8,128)(2,1)} %collective-permute-done.9.refs_1_, ...), custom_call_target="tpu_custom_call" | custom-call | flops 4294967296 | bytes 22020096 | tf_op jit(solution)/shard_map/rows_times_kv/pallas_call | solution.py:232
  142.7 7.4 %collective-permute-done.12 = bf16[128,4096]{1,0:T(8,128)(2,1)} collective-permute-done((bf16[128,4096]{1,0:T(8,128)(2,1)}, bf16[128,4096]{1,0:T(8,128)(2,1)}, u32[]{:S(2)}, u32[]{:S(2)}) %collective-permute-start.12) | collective-permute-done | bytes 1048608 | tf_op jit(solution)/shard_map/ppermute | solution.py:592
  151.8 4.6 %norm_rows.3 = (bf16[512,4096]{1,0:T(8,128)(2,1)}, f32[512,128]{1,0:T(8,128)S(1)}) custom-call(bf16[256,4096]{1,0:T(8,128)(2,1)S(1)} %copy-done.3, bf16[256,4096]{1,0:T(8,128)(2,1)S(1)} %copy-done.10, f32[1,4096]{1,0:T(1,128)S(1)} %bitcast.194), custom_call_target="tpu_custom_call" | custom-call | flops 8388608 | bytes 8667136 | tf_op jit(solution)/shard_map/norm_rows/pallas_call | solution.py:232
  159.6 3.2 constant_dynamic-slice_fusion.12
  162.8 8.5 %collective-permute-done.14 = bf16[1024,256]{1,0:T(8,128)(2,1)S(1)} collective-permute-done((bf16[1024,256]{1,0:T(8,128)(2,1)S(1)}, bf16[1024,256]{1,0:T(8,128)(2,1)S(1)}, u32[]{:S(2)}, u32[]{:S(2)}) %collective-permute-start.14) | collective-permute-done | bytes 524320 | tf_op jit(solution)/shard_map/ppermute | solution.py:592
  174.2 8.8 %rows_times_weight.2.q_ref = bf16[512,1024]{1,0:T(8,128)(2,1)S(1)} custom-call(s32[16]{0:T(128)S(1)} %stack.335.refs_0_, bf16[512,4096]{1,0:T(8,128)(2,1)S(1)} %copy-done.2, bf16[4096,1024]{1,0:T(8,128)(2,1)} %all-gather.3.cloned.1.call-done.refs_2_.refs_8_), custom_call_target="tpu_custom_call" | custom-call | flops 4294967296 | bytes 13631488 | tf_op jit(solution)/shard_map/rows_times_weight/pallas_call | solution.py:232
  183.1 11.9 %attention_forward.1 = (bf16[512,1024]{1,0:T(8,128)(2,1)S(1)}, f32[8,1,512]{2,1,0:T(1,128)S(1)}) custom-call(s32[2,8]{1,0:T(2,128)S(1)} %pad_add_fusion.1.bounds, bf16[512,1024]{1,0:T(8,128)(2,1)S(1)} %rows_times_weight.2.q_ref, bf16[2,1024,256]{2,1,0:T(8,128)(2,1)S(1)} %pad_maximum_fusion.8.kvp_ref, bf16[512,256]{1,0:T(8,128)(2,1)S(1)} %convolution_convert_fusion.kvl_ref), custom_call_target="tpu_custom_call" | custom-call | flops 2147483648 | bytes 3145728 | tf_op jit(solution)/shard_map/attention_forward/pallas_call | solution.py:163
  197.4 11.7 %weight_grad.2 = bf16[16,256,1024]{2,1,0:T(8,128)(2,1)} custom-call(s32[16]{0:T(128)S(1)} %stack.397.at, bf16[512,4096]{1,0:T(8,128)(2,1)S(1)} %bitcast.192, bf16[512,1024]{1,0:T(8,128)(2,1)S(1)} %get-tuple-element.92.heads_ref.refs_2_), custom_call_target="tpu_custom_call" | custom-call | flops 4294967296 | bytes 13631488 | tf_op jit(solution)/shard_map/weight_grad/pallas_call | solution.py:232
  209.4 2.2 copy-done.8
  211.6 9.5 %rows_times_weight.3.do_ref = bf16[512,1024]{1,0:T(8,128)(2,1)S(1)} custom-call(s32[16]{0:T(128)S(1)} %stack.335.refs_0_, bf16[512,4096]{1,0:T(8,128)(2,1)S(1)} %bitcast.193, bf16[4096,1024]{1,0:T(8,128)(2,1)} %all-gather.5.cloned.1.call-done.refs_2_.refs_3_), custom_call_target="tpu_custom_call" | custom-call | flops 4294967296 | bytes 13631488 | tf_op jit(solution)/shard_map/rows_times_weight/pallas_call | solution.py:232
  221.2 15.7 %attention_backward.1 = (bf16[512,1024]{1,0:T(8,128)(2,1)S(1)}, bf16[2,1024,256]{2,1,0:T(8,128)(2,1)S(1)}, bf16[512,256]{1,0:T(8,128)(2,1)S(1)}) custom-call(s32[2,8]{1,0:T(2,128)S(1)} %pad_add_fusion.1.bounds, bf16[512,1024]{1,0:T(8,128)(2,1)S(1)} %copy-done.19, bf16[512,1024]{1,0:T(8,128)(2,1)S(1)} %rows_times_weight.3.do_ref, ...), custom_call_target="tpu_custom_call" | custom-call | flops 5368709 | bytes 5242 | tf_op jit(solution)/shard_map/attention_backward/pallas_call | solution.py:195
  240.4 10.1 %heads_times_weight.1 = (bf16[2,128,1536]{2,1,0:T(8,128)(2,1)S(1)}, bf16[2,128,1536]{2,1,0:T(8,128)(2,1)S(1)}, bf16[2,128,2560]{2,1,0:T(8,128)(2,1)S(1)}, bf16[2,128,2560]{2,1,0:T(8,128)(2,1)S(1)}) custom-call(s32[16]{0:T(128)S(1)} %stack.335.refs_0_, s32[2]{0:T(128)S(1)} %pad_add_fusion.2.refs_1_.here, ...), custom_call_target="tpu_custom_call" | custom-call | flops 4294967 | bytes 13631 | tf_op jit(solution)/shard_map/heads_times_weight/pallas_call | solution.py:232
  258.6 14.3 %lat_back.1 = (bf16[2,128,2048]{2,1,0:T(8,128)(2,1)S(1)}, bf16[2,128,2048]{2,1,0:T(8,128)(2,1)S(1)}, bf16[2,128,2048]{2,1,0:T(8,128)(2,1)S(1)}, bf16[2,128,2048]{2,1,0:T(8,128)(2,1)S(1)}, f32[1,4096]{1,0:T(1,128)S(1)}) custom-call(s32[16]{0:T(128)S(1)} %stack.335.refs_0_, s32[2]{0:T(128)S(1)} %pad_add_fusion.2.refs_1_.here, ...), custom_call_target="tpu_custom_call" | custom-call | flops 5368709120 | bytes 20463616 | tf_op jit(solution)/shard_map/lat_back/pallas_call | solution.py:232
  274.9 8.3 %kv_weight_grad.2 = bf16[2,8,128,1024]{3,2,1,0:T(8,128)(2,1)S(1)} custom-call(s32[8]{0:T(128)S(1)} %stack.415.at, s32[2]{0:T(128)S(1)} %pad_add_fusion.2.refs_1_.here, bf16[512,4096]{1,0:T(8,128)(2,1)} %copy-done.1, bf16[512,1024]{1,0:T(8,128)(2,1)S(1)} %pad_maximum_fusion.11.d_kv_ref.d_ref, bf16[512,4096]{1,0:T(8,128)(2,1)} %get-tuple-element.125.refs_1_.lat_ref.act_ref, ...), custom_call_target="tpu_custom_call" | custom-call | flops 2684354560 | bytes 13893632 | tf_op jit(solution)/shard_map/kv_weight_grad/pallas_call | solution.py:232
  283.2 2.0 copy-done.6
  285.2 8.3 %kv_weight_grad.3 = bf16[2,8,128,1024]{3,2,1,0:T(8,128)(2,1)S(1)} custom-call(s32[8]{0:T(128)S(1)} %stack.406.at, s32[2]{0:T(128)S(1)} %pad_add_fusion.2.refs_1_.here, bf16[512,4096]{1,0:T(8,128)(2,1)} %copy-done.1, bf16[512,1024]{1,0:T(8,128)(2,1)S(1)} %pad_maximum_fusion.11.d_kv_ref.d_ref, bf16[512,4096]{1,0:T(8,128)(2,1)} %get-tuple-element.125.refs_1_.lat_ref.act_ref, ...), custom_call_target="tpu_custom_call" | custom-call | flops 2684354560 | bytes 13893632 | tf_op jit(solution)/shard_map/kv_weight_grad/pallas_call | solution.py:232
  295.8 10.1 %weight_grad.3 = bf16[8,256,2048]{2,1,0:T(8,128)(2,1)} custom-call(s32[8]{0:T(128)S(1)} %stack.416.at, bf16[512,4096]{1,0:T(8,128)(2,1)} %get-tuple-element.125.refs_1_.lat_ref.act_ref, bf16[512,2048]{1,0:T(8,128)(2,1)S(1)} %pad_maximum_fusion.4.heads_ref), custom_call_target="tpu_custom_call" | custom-call | flops 4294967296 | bytes 14680064 | tf_op jit(solution)/shard_map/weight_grad/pallas_call | solution.py:232
  307.7 5.7 %collective-permute-done.19 = bf16[2,2,4,128,1024]{4,3,2,1,0:T(8,128)(2,1)} collective-permute-done((bf16[2,2,4,128,1024]{4,3,2,1,0:T(8,128)(2,1)}, bf16[2,2,4,128,1024]{4,3,2,1,0:T(8,128)(2,1)}, u32[]{:S(2)}, u32[]{:S(2)}) %collective-permute-start.19) | collective-permute-done | bytes 4194336 | tf_op jit(solution)/shard_map/ppermute | solution.py:589
  313.5 2.0 fusion.9
  316.1 2.0 fusion.10
  322.9 18.2 %ctx_back.1 = (f32[512,4096]{1,0:T(8,128)}, f32[1,4096]{1,0:T(1,128)S(1)}) custom-call(bf16[512,1024]{1,0:T(8,128)(2,1)S(1)} %pad_maximum_fusion.11.d_kv_ref.d_ref, bf16[4096,1024]{1,0:T(8,128)(2,1)} %get-tuple-element.83.kv_ref, bf16[512,4096]{1,0:T(8,128)(2,1)S(1)} %copy-done.5, f32[512,128]{1,0:T(8,128)S(1)} %copy-done.36, f32[1,4096]{1,0:T(1,128)S(1)} %bitcast.196), custom_call_target="tpu_custom_call" | custom-call | flops 4294967296 | bytes 22315008 | tf_op jit(solution)/shard_map/ctx_back/pallas_call | solution.py:232
  341.1 10.6 %collective-permute-done.20 = bf16[128,1536]{1,0:T(8,128)(2,1)S(1)} collective-permute-done((bf16[128,1536]{1,0:T(8,128)(2,1)S(1)}, bf16[128,1536]{1,0:T(8,128)(2,1)S(1)}, u32[]{:S(2)}, u32[]{:S(2)}) %collective-permute-start.20) | collective-permute-done | bytes 393248 | tf_op jit(solution)/shard_map/ppermute | solution.py:595
  352.9 3.9 bitcast_add_fusion
  359.3 2.0 collective-permute-start.34
  361.4 2.4 bitcast_add_fusion.2
  366.4 5.4 %collective-permute-done.26 = bf16[4,128,512]{2,1,0:T(8,128)(2,1)S(1)} collective-permute-done((bf16[4,128,512]{2,1,0:T(8,128)(2,1)S(1)}, bf16[4,128,512]{2,1,0:T(8,128)(2,1)S(1)}, u32[]{:S(2)}, u32[]{:S(2)}) %collective-permute-start.26) | collective-permute-done | bytes 524320 | tf_op jit(solution)/shard_map/ppermute | solution.py:595
  374.6 19.7 %collective-permute-done.25 = bf16[2,128,2048]{2,1,0:T(8,128)(2,1)S(1)} collective-permute-done((bf16[2,128,2048]{2,1,0:T(8,128)(2,1)S(1)}, bf16[2,128,2048]{2,1,0:T(8,128)(2,1)S(1)}, u32[]{:S(2)}, u32[]{:S(2)}) %collective-permute-start.25) | collective-permute-done | bytes 1048608 | tf_op jit(solution)/shard_map/ppermute | solution.py:592
  399.9 2.0 collective-permute-start.40
  403.0 7.0 %collective-permute-done.36 = f32[2,128]{1,0:T(2,128)S(1)} collective-permute-done((f32[2,128]{1,0:T(2,128)S(1)}, f32[2,128]{1,0:T(2,128)S(1)}, u32[]{:S(2)}, u32[]{:S(2)}) %collective-permute-start.36) | collective-permute-done | bytes 1056 | tf_op jit(solution)/shard_map/ppermute | solution.py:592
  414.6 7.6 %collective-permute-done.29 = bf16[128,2048]{1,0:T(8,128)(2,1)S(1)} collective-permute-done((bf16[128,2048]{1,0:T(8,128)(2,1)}, bf16[128,2048]{1,0:T(8,128)(2,1)S(1)}, u32[]{:S(2)}, u32[]{:S(2)}) %collective-permute-start.29) | collective-permute-done | bytes 524320 | tf_op jit(solution)/shard_map/ppermute | solution.py:595
  425.0 2.5 fusion.6
  428.9 2.8 convert_element_type.254
  431.8 2.0 convert_add_fusion.1
  (273 shorter events, 81.4 us)
Async XLA Ops:
  7.2 116.8 %all-gather.3.cloned.1.call-start = ((), (), s32[]{:S(2)}) async-start(), calls=%async_computation.2 | async-start | bytes 9437184 | tf_op jit(solution)/shard_map/all_gather | solution.py:673
  9.4 15.9 %collective-permute-start.4 = (bf16[256,1024]{1,0:T(8,128)(2,1)}, bf16[256,1024]{1,0:T(8,128)(2,1)S(1)}, u32[]{:S(2)}, u32[]{:S(2)}) collective-permute-start(bf16[256,1024]{1,0:T(8,128)(2,1)} %get-tuple-element.164), channel_id=1, source_target_pairs={{0,4},{2,6},{4,0},{6,2},{8,12},{10,14},{12,8},{14,10},{16,20},{18,... | collective-permute-start | bytes 1572872 | tf_op jit(solution)/shard_map/ppermute | solution.py:592
  13.4 27.9 %collective-permute-start.5 = (bf16[256,1024]{1,0:T(8,128)(2,1)}, bf16[256,1024]{1,0:T(8,128)(2,1)}, u32[]{:S(2)}, u32[]{:S(2)}) collective-permute-start(bf16[256,1024]{1,0:T(8,128)(2,1)} %get-tuple-element.158), channel_id=1, source_target_pairs={{0,4},{2,6},{4,0},{6,2},{8,12},{10,14},{12,8},{14,10},{16,20},{18,... | collective-permute-start | bytes 1572872 | tf_op jit(solution)/shard_map/ppermute | solution.py:592
  15.1 20.7 %collective-permute-start.3 = (bf16[128,1024]{1,0:T(8,128)(2,1)}, bf16[128,1024]{1,0:T(8,128)(2,1)}, u32[]{:S(2)}, u32[]{:S(2)}) collective-permute-start(bf16[128,1024]{1,0:T(8,128)(2,1)} %get-tuple-element.133), channel_id=1, source_target_pairs={{0,24},{2,26},{4,28},{6,30},{8,0},{10,2},{12,4},{14,6},{16,8},{18,... | collective-permute-start | bytes 786440 | tf_op jit(solution)/shard_map/ppermute | solution.py:601
  19.3 22.1 %collective-permute-start.2 = (bf16[128,1024]{1,0:T(8,128)(2,1)}, bf16[128,1024]{1,0:T(8,128)(2,1)}, u32[]{:S(2)}, u32[]{:S(2)}) collective-permute-start(bf16[128,1024]{1,0:T(8,128)(2,1)} %get-tuple-element.133), channel_id=1, source_target_pairs={{0,16},{2,18},{4,20},{6,22},{8,24},{10,26},{12,28},{14,30},{16,0},... | collective-permute-start | bytes 786440 | tf_op jit(solution)/shard_map/ppermute | solution.py:601
  19.3 22.1 %collective-permute-start.1 = (bf16[128,1024]{1,0:T(8,128)(2,1)}, bf16[128,1024]{1,0:T(8,128)(2,1)}, u32[]{:S(2)}, u32[]{:S(2)}) collective-permute-start(bf16[128,1024]{1,0:T(8,128)(2,1)} %get-tuple-element.133), channel_id=1, source_target_pairs={{0,8},{2,10},{4,12},{6,14},{8,16},{10,18},{12,20},{14,22},{16,24},... | collective-permute-start | bytes 786440 | tf_op jit(solution)/shard_map/ppermute | solution.py:601
  25.3 10.5 %collective-permute-start = (s32[1,4]{1,0:T(1,128)S(1)}, s32[1,4]{1,0:T(1,128)S(1)}, u32[]{:S(2)}, u32[]{:S(2)}) collective-permute-start(s32[1,4]{1,0:T(1,128)S(1)} %copy-done.62), channel_id=1, source_target_pairs={{0,4},{2,6},{4,0},{6,2},{8,12},{10,14},{12,8},{14,10},{16,20},{18,... | collective-permute-start | bytes 56 | tf_op jit(solution)/shard_map/ppermute | solution.py:592
  41.4 168.0 %all-gather.5.cloned.1.call-start = ((), (), s32[]{:S(2)}) async-start(), calls=%async_computation.3 | async-start | bytes 9437184 | tf_op jit(solution)/shard_map/all_gather | solution.py:673
  42.7 23.5 %collective-permute-start.6 = (bf16[512,1024]{1,0:T(8,128)(2,1)S(1)}, bf16[512,1024]{1,0:T(8,128)(2,1)S(1)}, u32[]{:S(2)}, u32[]{:S(2)}) collective-permute-start(bf16[512,1024]{1,0:T(8,128)(2,1)S(1)} %pad_maximum_fusion.6), channel_id=1, source_target_pairs={{0,4},{2,6},{4,0},{6,2},{8,12},{10,14},{12,8},{14,10},{16,20},{18,... | collective-permute-start | bytes 3145736 | tf_op jit(solution)/shard_map/ppermute | solution.py:592
  44.3 23.1 %collective-permute-start.7 = (bf16[128,4096]{1,0:T(8,128)(2,1)S(1)}, bf16[128,4096]{1,0:T(8,128)(2,1)S(1)}, u32[]{:S(2)}, u32[]{:S(2)}) collective-permute-start(bf16[128,4096]{1,0:T(8,128)(2,1)S(1)} %copy-done.44), channel_id=1, source_target_pairs={{0,1},{1,0},{2,3},{3,2},{4,5},{5,4},{6,7},{7,6},{8,9},{9,8},{10,11... | collective-permute-start | bytes 3145736 | tf_op jit(solution)/shard_map/ppermute | solution.py:595
  50.0 63.9 %copy-start.49 = (bf16[256,1024]{1,0:T(8,128)(2,1)S(1)}, bf16[256,1024]{1,0:T(8,128)(2,1)}, u32[]{:S(2)}) copy-start(bf16[256,1024]{1,0:T(8,128)(2,1)} %get-tuple-element.157) | copy-start | bytes 1572868
  57.8 58.2 %copy-start.35 = (f32[512,128]{1,0:T(8,128)}, f32[512,128]{1,0:T(8,128)S(1)}, u32[]{:S(2)}) copy-start(f32[512,128]{1,0:T(8,128)S(1)} %get-tuple-element.110.scale_ref) | copy-start | bytes 786436
  67.4 44.9 %collective-permute-start.8 = (bf16[256,4096]{1,0:T(8,128)(2,1)S(1)}, bf16[256,4096]{1,0:T(8,128)(2,1)S(1)}, u32[]{:S(2)}, u32[]{:S(2)}) collective-permute-start(bf16[256,4096]{1,0:T(8,128)(2,1)S(1)} %copy-done.3), channel_id=1, source_target_pairs={{0,4},{2,6},{4,0},{6,2},{8,12},{10,14},{12,8},{14,10},{16,20},{18,... | collective-permute-start | bytes 6291464 | tf_op jit(solution)/shard_map/ppermute | solution.py:592
  68.8 45.1 %collective-permute-start.9 = (bf16[1024,1024]{1,0:T(8,128)(2,1)}, bf16[1024,1024]{1,0:T(8,128)(2,1)}, u32[]{:S(2)}, u32[]{:S(2)}) collective-permute-start(bf16[1024,1024]{1,0:T(8,128)(2,1)} %constant_dynamic-update-slice_fusion.refs_0_), channel_id=1, source_target_pairs={{0,1},{1,0},{2,3},{3,2},{4,5},{5,4},{6,7},{7,6},{8,9},{9,8},{10,11... | collective-permute-start | bytes 6291464 | tf_op jit(solution)/shard_map/ppermute | solution.py:595
  70.3 45.7 %collective-permute-start.10 = (bf16[1024,1024]{1,0:T(8,128)(2,1)}, bf16[1024,1024]{1,0:T(8,128)(2,1)}, u32[]{:S(2)}, u32[]{:S(2)}) collective-permute-start(bf16[1024,1024]{1,0:T(8,128)(2,1)} %constant_dynamic-update-slice_fusion.refs_0_), channel_id=1, source_target_pairs={{0,2},{2,0},{4,6},{6,4},{8,10},{10,8},{12,14},{14,12},{16,18},{18,... | collective-permute-start | bytes 6291464 | tf_op jit(solution)/shard_map/ppermute | solution.py:589
  113.9 4.5 %collective-permute-start.11 = (bf16[1024,1024]{1,0:T(8,128)(2,1)}, bf16[1024,1024]{1,0:T(8,128)(2,1)}, u32[]{:S(2)}, u32[]{:S(2)}) collective-permute-start(bf16[1024,1024]{1,0:T(8,128)(2,1)} %collective-permute-done.9.refs_1_), channel_id=1, source_target_pairs={{0,2},{2,0},{4,6},{6,4},{8,10},{10,8},{12,14},{14,12},{16,18},{18,... | collective-permute-start | bytes 6291464 | tf_op jit(solution)/shard_map/ppermute | solution.py:589
  124.0 275.1 %reduce-scatter.5.cloned.1.call-start = ((), (), s32[]{:S(2)}) async-start(), calls=%async_computation.5 | async-start | bytes 9437184 | tf_op jit(solution)/shard_map/reduce_scatter | solution.py:747
  124.4 25.7 %collective-permute-start.12 = (bf16[128,4096]{1,0:T(8,128)(2,1)}, bf16[128,4096]{1,0:T(8,128)(2,1)}, u32[]{:S(2)}, u32[]{:S(2)}) collective-permute-start(bf16[128,4096]{1,0:T(8,128)(2,1)} %copy-done.58), channel_id=1, source_target_pairs={{0,4},{2,6},{4,0},{6,2},{8,12},{10,14},{12,8},{14,10},{16,20},{18,... | collective-permute-start | bytes 3145736 | tf_op jit(solution)/shard_map/ppermute | solution.py:592
  140.6 15.7 %collective-permute-start.13 = (bf16[512,512]{1,0:T(8,128)(2,1)}, bf16[512,512]{1,0:T(8,128)(2,1)}, u32[]{:S(2)}, u32[]{:S(2)}) collective-permute-start(bf16[512,512]{1,0:T(8,128)(2,1)} %constant_dynamic-slice_fusion.13), channel_id=1, source_target_pairs={{0,1},{1,0},{2,3},{3,2},{4,5},{5,4},{6,7},{7,6},{8,9},{9,8},{10,11... | collective-permute-start | bytes 1572872 | tf_op jit(solution)/shard_map/ppermute | solution.py:595
  158.0 13.3 %collective-permute-start.14 = (bf16[1024,256]{1,0:T(8,128)(2,1)S(1)}, bf16[1024,256]{1,0:T(8,128)(2,1)S(1)}, u32[]{:S(2)}, u32[]{:S(2)}) collective-permute-start(bf16[1024,256]{1,0:T(8,128)(2,1)S(1)} %pad_maximum_fusion.13), channel_id=1, source_target_pairs={{0,4},{2,6},{4,0},{6,2},{8,12},{10,14},{12,8},{14,10},{16,20},{18,... | collective-permute-start | bytes 1572872 | tf_op jit(solution)/shard_map/ppermute | solution.py:592
  171.3 23.7 %collective-permute-start.15 = (bf16[128,4096]{1,0:T(8,128)(2,1)S(1)}, bf16[128,4096]{1,0:T(8,128)(2,1)S(1)}, u32[]{:S(2)}, u32[]{:S(2)}) collective-permute-start(bf16[128,4096]{1,0:T(8,128)(2,1)S(1)} %copy-done.45), channel_id=1, source_target_pairs={{0,4},{2,6},{4,0},{6,2},{8,12},{10,14},{12,8},{14,10},{16,20},{18,... | collective-permute-start | bytes 3145736 | tf_op jit(solution)/shard_map/ppermute | solution.py:592
  209.2 219.8 %reduce-scatter.3.cloned.1.call-start = ((), (), s32[]{:S(2)}) async-start(), calls=%async_computation.4 | async-start | bytes 9437184 | tf_op jit(solution)/shard_map/reduce_scatter | solution.py:731
  238.7 11.9 %collective-permute-start.16 = (bf16[1024,256]{1,0:T(8,128)(2,1)}, bf16[1024,256]{1,0:T(8,128)(2,1)S(1)}, u32[]{:S(2)}, u32[]{:S(2)}) collective-permute-start(bf16[1024,256]{1,0:T(8,128)(2,1)} %slice_bitcast_fusion.4), channel_id=1, source_target_pairs={{0,4},{2,6},{4,0},{6,2},{8,12},{10,14},{12,8},{14,10},{16,20},{18,... | collective-permute-start | bytes 1572872 | tf_op jit(solution)/shard_map/ppermute | solution.py:592
  252.1 20.9 %collective-permute-start.18 = (bf16[512,512]{1,0:T(8,128)(2,1)S(1)}, bf16[512,512]{1,0:T(8,128)(2,1)S(1)}, u32[]{:S(2)}, u32[]{:S(2)}) collective-permute-start(bf16[512,512]{1,0:T(8,128)(2,1)S(1)} %dynamic-slice_bitcast_fusion), channel_id=1, source_target_pairs={{0,1},{1,0},{2,3},{3,2},{4,5},{5,4},{6,7},{7,6},{8,9},{9,8},{10,11... | collective-permute-start | bytes 1572872 | tf_op jit(solution)/shard_map/ppermute | solution.py:595
  255.2 40.5 %collective-permute-start.17 = (bf16[2,128,1536]{2,1,0:T(8,128)(2,1)S(1)}, bf16[2,128,1536]{2,1,0:T(8,128)(2,1)S(1)}, u32[]{:S(2)}, u32[]{:S(2)}) collective-permute-start(bf16[2,128,1536]{2,1,0:T(8,128)(2,1)S(1)} %get-tuple-element.96), channel_id=1, source_target_pairs={{0,4},{2,6},{4,0},{6,2},{8,12},{10,14},{12,8},{14,10},{16,20},{18,... | collective-permute-start | bytes 2359304 | tf_op jit(solution)/shard_map/ppermute | solution.py:592
  255.8 37.7 %collective-permute-start.37 = (bf16[512,1024]{1,0:T(8,128)(2,1)S(1)}, bf16[512,1024]{1,0:T(8,128)(2,1)S(1)}, u32[]{:S(2)}, u32[]{:S(2)}) collective-permute-start(bf16[512,1024]{1,0:T(8,128)(2,1)S(1)} %get-tuple-element.126.refs_2_), channel_id=1, source_target_pairs={{0,4},{2,6},{4,0},{6,2},{8,12},{10,14},{12,8},{14,10},{16,20},{18,... | collective-permute-start | bytes 3145736 | tf_op jit(solution)/shard_map/ppermute | solution.py:592
  257.2 38.5 %collective-permute-start.21 = (bf16[2,128,2560]{2,1,0:T(8,128)(2,1)S(1)}, bf16[2,128,2560]{2,1,0:T(8,128)(2,1)S(1)}, u32[]{:S(2)}, u32[]{:S(2)}) collective-permute-start(bf16[2,128,2560]{2,1,0:T(8,128)(2,1)S(1)} %get-tuple-element.107), channel_id=1, source_target_pairs={{0,1},{1,0},{2,3},{3,2},{4,5},{5,4},{6,7},{7,6},{8,9},{9,8},{10,11... | collective-permute-start | bytes 3932168 | tf_op jit(solution)/shard_map/ppermute | solution.py:595
  305.9 7.6 %collective-permute-start.19 = (bf16[2,2,4,128,1024]{4,3,2,1,0:T(8,128)(2,1)}, bf16[2,2,4,128,1024]{4,3,2,1,0:T(8,128)(2,1)}, u32[]{:S(2)}, u32[]{:S(2)}) collective-permute-start(bf16[2,2,4,128,1024]{4,3,2,1,0:T(8,128)(2,1)} %bitcast.191), channel_id=1, source_target_pairs={{0,2},{2,0},{4,6},{6,4},{8,10},{10,8},{12,14},{14,12},{16,18},{18,... | collective-permute-start | bytes 12582920 | tf_op jit(solution)/shard_map/ppermute | solution.py:589
  315.5 37.1 %collective-permute-start.23 = (bf16[2,4,128,512]{3,2,1,0:T(8,128)(2,1)S(1)}, bf16[2,4,128,512]{3,2,1,0:T(8,128)(2,1)}, u32[]{:S(2)}, u32[]{:S(2)}) collective-permute-start(bf16[2,4,128,512]{3,2,1,0:T(8,128)(2,1)S(1)} %fusion.9), channel_id=1, source_target_pairs={{0,4},{2,6},{4,0},{6,2},{8,12},{10,14},{12,8},{14,10},{16,20},{18,... | collective-permute-start | bytes 3145736 | tf_op jit(solution)/shard_map/ppermute | solution.py:592
  318.1 34.5 %collective-permute-start.24 = (bf16[2,4,128,512]{3,2,1,0:T(8,128)(2,1)S(1)}, bf16[2,4,128,512]{3,2,1,0:T(8,128)(2,1)}, u32[]{:S(2)}, u32[]{:S(2)}) collective-permute-start(bf16[2,4,128,512]{3,2,1,0:T(8,128)(2,1)S(1)} %fusion.10), channel_id=1, source_target_pairs={{0,1},{1,0},{2,3},{3,2},{4,5},{5,4},{6,7},{7,6},{8,9},{9,8},{10,11... | collective-permute-start | bytes 3145736 | tf_op jit(solution)/shard_map/ppermute | solution.py:595
  319.1 32.5 %collective-permute-start.20 = (bf16[128,1536]{1,0:T(8,128)(2,1)S(1)}, bf16[128,1536]{1,0:T(8,128)(2,1)S(1)}, u32[]{:S(2)}, u32[]{:S(2)}) collective-permute-start(bf16[128,1536]{1,0:T(8,128)(2,1)S(1)} %fusion.20), channel_id=1, source_target_pairs={{0,1},{1,0},{2,3},{3,2},{4,5},{5,4},{6,7},{7,6},{8,9},{9,8},{10,11... | collective-permute-start | bytes 1179656 | tf_op jit(solution)/shard_map/ppermute | solution.py:595
  321.4 35.6 %collective-permute-start.22 = (bf16[128,2560]{1,0:T(8,128)(2,1)}, bf16[128,2560]{1,0:T(8,128)(2,1)}, u32[]{:S(2)}, u32[]{:S(2)}) collective-permute-start(bf16[128,2560]{1,0:T(8,128)(2,1)} %fusion.13), channel_id=1, source_target_pairs={{0,4},{2,6},{4,0},{6,2},{8,12},{10,14},{12,8},{14,10},{16,20},{18,... | collective-permute-start | bytes 1966088 | tf_op jit(solution)/shard_map/ppermute | solution.py:592
  352.8 6.4 %collective-permute-start.31 = (f32[2,4,2,2,128]{4,3,2,0,1:T(2,128)S(1)}, f32[2,4,2,2,128]{4,3,2,0,1:T(2,128)S(1)}, u32[]{:S(2)}, u32[]{:S(2)}) collective-permute-start(f32[2,4,2,2,128]{4,3,2,0,1:T(2,128)S(1)} %bitcast.206), channel_id=1, source_target_pairs={{0,2},{2,0},{4,6},{6,4},{8,10},{10,8},{12,14},{14,12},{16,18},{18,... | collective-permute-start | bytes 49160 | tf_op jit(solution)/shard_map/ppermute | solution.py:589
  357.0 14.8 %collective-permute-start.26 = (bf16[4,128,512]{2,1,0:T(8,128)(2,1)S(1)}, bf16[4,128,512]{2,1,0:T(8,128)(2,1)S(1)}, u32[]{:S(2)}, u32[]{:S(2)}) collective-permute-start(bf16[4,128,512]{2,1,0:T(8,128)(2,1)S(1)} %fusion.16), channel_id=1, source_target_pairs={{0,1},{1,0},{2,3},{3,2},{4,5},{5,4},{6,7},{7,6},{8,9},{9,8},{10,11... | collective-permute-start | bytes 1572872 | tf_op jit(solution)/shard_map/ppermute | solution.py:595
  357.8 14.8 %collective-permute-start.27 = (bf16[4,128,512]{2,1,0:T(8,128)(2,1)S(1)}, bf16[4,128,512]{2,1,0:T(8,128)(2,1)S(1)}, u32[]{:S(2)}, u32[]{:S(2)}) collective-permute-start(bf16[4,128,512]{2,1,0:T(8,128)(2,1)S(1)} %fusion.17), channel_id=1, source_target_pairs={{0,4},{2,6},{4,0},{6,2},{8,12},{10,14},{12,8},{14,10},{16,20},{18,... | collective-permute-start | bytes 1572872 | tf_op jit(solution)/shard_map/ppermute | solution.py:592
  359.2 4.6 %collective-permute-start.32 = (f32[2,2,2,128]{3,2,1,0:T(2,128)S(1)}, f32[2,2,2,128]{3,2,1,0:T(2,128)S(1)}, u32[]{:S(2)}, u32[]{:S(2)}) collective-permute-start(f32[2,2,2,128]{3,2,1,0:T(2,128)S(1)} %get-tuple-element.171), channel_id=1, source_target_pairs={{0,24},{2,26},{4,28},{6,30},{8,0},{10,2},{12,4},{14,6},{16,8},{18,... | collective-permute-start | bytes 12296 | tf_op jit(solution)/shard_map/ppermute | solution.py:601
  359.3 5.7 %collective-permute-start.34 = (f32[2,2,2,128]{3,2,1,0:T(2,128)S(1)}, f32[2,2,2,128]{3,2,1,0:T(2,128)S(1)}, u32[]{:S(2)}, u32[]{:S(2)}) collective-permute-start(f32[2,2,2,128]{3,2,1,0:T(2,128)S(1)} %get-tuple-element.172), channel_id=1, source_target_pairs={{0,8},{2,10},{4,12},{6,14},{8,16},{10,18},{12,20},{14,22},{16,24},... | collective-permute-start | bytes 12296 | tf_op jit(solution)/shard_map/ppermute | solution.py:601
  361.3 5.1 %collective-permute-start.33 = (f32[2,2,2,128]{3,2,1,0:T(2,128)S(1)}, f32[2,2,2,128]{3,2,1,0:T(2,128)S(1)}, u32[]{:S(2)}, u32[]{:S(2)}) collective-permute-start(f32[2,2,2,128]{3,2,1,0:T(2,128)S(1)} %get-tuple-element.173), channel_id=1, source_target_pairs={{0,16},{2,18},{4,20},{6,22},{8,24},{10,26},{12,28},{14,30},{16,0},... | collective-permute-start | bytes 12296 | tf_op jit(solution)/shard_map/ppermute | solution.py:601
  363.8 30.5 %collective-permute-start.25 = (bf16[2,128,2048]{2,1,0:T(8,128)(2,1)S(1)}, bf16[2,128,2048]{2,1,0:T(8,128)(2,1)S(1)}, u32[]{:S(2)}, u32[]{:S(2)}) collective-permute-start(bf16[2,128,2048]{2,1,0:T(8,128)(2,1)S(1)} %copy-done.34), channel_id=1, source_target_pairs={{0,4},{2,6},{4,0},{6,2},{8,12},{10,14},{12,8},{14,10},{16,20},{18,... | collective-permute-start | bytes 3145736 | tf_op jit(solution)/shard_map/ppermute | solution.py:592
  365.0 29.3 %collective-permute-start.28 = (bf16[2,128,2048]{2,1,0:T(8,128)(2,1)S(1)}, bf16[2,128,2048]{2,1,0:T(8,128)(2,1)S(1)}, u32[]{:S(2)}, u32[]{:S(2)}) collective-permute-start(bf16[2,128,2048]{2,1,0:T(8,128)(2,1)S(1)} %copy-done.32), channel_id=1, source_target_pairs={{0,1},{1,0},{2,3},{3,2},{4,5},{5,4},{6,7},{7,6},{8,9},{9,8},{10,11... | collective-permute-start | bytes 3145736 | tf_op jit(solution)/shard_map/ppermute | solution.py:595
  394.4 4.8 %collective-permute-start.35 = (f32[2,2,128]{2,1,0:T(2,128)S(1)}, f32[2,2,128]{2,1,0:T(2,128)S(1)}, u32[]{:S(2)}, u32[]{:S(2)}) collective-permute-start(f32[2,2,128]{2,1,0:T(2,128)S(1)} %bitcast.209), channel_id=1, source_target_pairs={{0,1},{1,0},{2,3},{3,2},{4,5},{5,4},{6,7},{7,6},{8,9},{9,8},{10,11... | collective-permute-start | bytes 6152 | tf_op jit(solution)/shard_map/ppermute | solution.py:595
  396.7 15.1 %collective-permute-start.30 = (bf16[128,2048]{1,0:T(8,128)(2,1)}, bf16[128,2048]{1,0:T(8,128)(2,1)}, u32[]{:S(2)}, u32[]{:S(2)}) collective-permute-start(bf16[128,2048]{1,0:T(8,128)(2,1)} %fusion.15), channel_id=1, source_target_pairs={{0,4},{2,6},{4,0},{6,2},{8,12},{10,14},{12,8},{14,10},{16,20},{18,... | collective-permute-start | bytes 1572872 | tf_op jit(solution)/shard_map/ppermute | solution.py:592
  399.1 10.8 %collective-permute-start.36 = (f32[2,128]{1,0:T(2,128)S(1)}, f32[2,128]{1,0:T(2,128)S(1)}, u32[]{:S(2)}, u32[]{:S(2)}) collective-permute-start(f32[2,128]{1,0:T(2,128)S(1)} %bitcast.210), channel_id=1, source_target_pairs={{0,4},{2,6},{4,0},{6,2},{8,12},{10,14},{12,8},{14,10},{16,20},{18,... | collective-permute-start | bytes 3080 | tf_op jit(solution)/shard_map/ppermute | solution.py:592
  399.7 32.1 %collective-permute-start.38 = (bf16[128,1024]{1,0:T(8,128)(2,1)}, bf16[128,1024]{1,0:T(8,128)(2,1)S(1)}, u32[]{:S(2)}, u32[]{:S(2)}) collective-permute-start(bf16[128,1024]{1,0:T(8,128)(2,1)} %get-tuple-element.128), channel_id=1, source_target_pairs={{0,24},{2,26},{4,28},{6,30},{8,0},{10,2},{12,4},{14,6},{16,8},{18,... | collective-permute-start | bytes 786440 | tf_op jit(solution)/shard_map/ppermute | solution.py:601
  399.8 32.0 %collective-permute-start.39 = (bf16[128,1024]{1,0:T(8,128)(2,1)}, bf16[128,1024]{1,0:T(8,128)(2,1)}, u32[]{:S(2)}, u32[]{:S(2)}) collective-permute-start(bf16[128,1024]{1,0:T(8,128)(2,1)} %get-tuple-element.129), channel_id=1, source_target_pairs={{0,16},{2,18},{4,20},{6,22},{8,24},{10,26},{12,28},{14,30},{16,0},... | collective-permute-start | bytes 786440 | tf_op jit(solution)/shard_map/ppermute | solution.py:601
  399.9 31.9 %collective-permute-start.40 = (bf16[128,1024]{1,0:T(8,128)(2,1)}, bf16[128,1024]{1,0:T(8,128)(2,1)}, u32[]{:S(2)}, u32[]{:S(2)}) collective-permute-start(bf16[128,1024]{1,0:T(8,128)(2,1)} %get-tuple-element.130), channel_id=1, source_target_pairs={{0,8},{2,10},{4,12},{6,14},{8,16},{10,18},{12,20},{14,22},{16,24},... | collective-permute-start | bytes 786440 | tf_op jit(solution)/shard_map/ppermute | solution.py:601
  410.0 12.3 %collective-permute-start.29 = (bf16[128,2048]{1,0:T(8,128)(2,1)}, bf16[128,2048]{1,0:T(8,128)(2,1)S(1)}, u32[]{:S(2)}, u32[]{:S(2)}) collective-permute-start(bf16[128,2048]{1,0:T(8,128)(2,1)} %fusion.14), channel_id=1, source_target_pairs={{0,1},{1,0},{2,3},{3,2},{4,5},{5,4},{6,7},{7,6},{8,9},{9,8},{10,11... | collective-permute-start | bytes 1572872 | tf_op jit(solution)/shard_map/ppermute | solution.py:595
  411.7 12.1 %collective-permute-start.41 = (bf16[256,1024]{1,0:T(8,128)(2,1)S(1)}, bf16[256,1024]{1,0:T(8,128)(2,1)S(1)}, u32[]{:S(2)}, u32[]{:S(2)}) collective-permute-start(bf16[256,1024]{1,0:T(8,128)(2,1)S(1)} %split.7), channel_id=1, source_target_pairs={{0,4},{2,6},{4,0},{6,2},{8,12},{10,14},{12,8},{14,10},{16,20},{18,... | collective-permute-start | bytes 1572872 | tf_op jit(solution)/shard_map/ppermute | solution.py:592
  (61 other events, 480.6 us)
Sparse Core Ops, SparseCore 0:
  41.5 82.4 all-gather.2
  125.6 80.5 all-gather.4
  209.3 88.0 reduce-scatter.4
  306.0 86.3 reduce-scatter.2
where the time goes:
time: 441 us; the launch traced here: 440 us
  waiting for transfers between devices  151 us (34%)
  Pallas kernels  150 us (34%)
  starting transfers between devices  48.2 us (11%)
  other arithmetic  38.6 us (9%)
  local copies, waits for them, and re-layouts  37.1 us (8%)
  between operations  15 us (3%)
    pallas_call x12, Pallas kernels, call(): pl.pallas_call(kernel, grid_spec=pltpu.PrefetchScalarGridSpec(num_scalar_...  122 us
    ppermute x18, waiting for transfers between devices, over_y(): return lax.ppermute(v, 'dp', self.perm_y)  107 us
    unnamed x130, local copies, waits for them, and re-layouts  24.2 us
    ppermute x11, waiting for transfers between devices, over_x(): return lax.ppermute(v, 'tensor', [(0, 1), (1, 0)])  24 us
    ppermute x18, starting transfers between devices, over_y(): return lax.ppermute(v, 'dp', self.perm_y)  23.9 us
    pallas_call x1, Pallas kernels, attend_back(): pl.pallas_call(bwd_kernel, grid_spec=pltpu.PrefetchScalarGridSpec(num_sca...  15.7 us
    ppermute x11, starting transfers between devices, over_x(): return lax.ppermute(v, 'tensor', [(0, 1), (1, 0)])  14.3 us
    pallas_call x1, Pallas kernels, attend(): pl.pallas_call(fwd_kernel, grid_spec=pltpu.PrefetchScalarGridSpec(num_sca...  11.9 us
  transfers between devices with their start and end apart: 46, of which 20 were waited for; matrix products, arithmetic and copies ran while one was open for 12% of the time, Pallas kernels for 34%

commit v1 on v0

--- a/solution.py
+++ b/solution.py
@@ -954,7 +954,8 @@
     q_part, q_weight_grad = scatter_rows_of_y(
         here, after(lat_n, kv_sum.own_part, *branch.first), d_queries_all
     )
-    kv_sum.start()
+    out_weight_grad, out_last = out_result(q_part)
+    kv_sum.start(out_last)
     branch.prepare(*kv_sum.sent)
     branch.finish()
     context_grad, ctx_gain_part = ctx_back(
@@ -970,7 +971,6 @@
     kv_weight_grad = kv_sum.result(third, q_weight_grad)
     lat_sum.prepare()
     lat_sum.finish(third, third)
-    out_weight_grad, _ = out_result(*third)
     gains = scatter_gains(here, after(gains, *third))
     lat_mine = lax.dynamic_slice_in_dim(latents, here.x * my_rows, my_rows, 0).astype(full)
     resampled = (lat_mine + branch.result()).astype(low)

time: 441 us -> 440 us (level)
    ppermute x18, waiting for transfers between devices: 107 us -> 123 us  [over_y(): return lax.ppermute(v, 'dp', self.perm_y)]
    ppermute x11, waiting for transfers between devices: 24 us -> 16.8 us  [over_x(): return lax.ppermute(v, 'tensor', [(0, 1), (1, 0)])]
    ppermute x4, waiting for transfers between devices: 8.1 us -> 2.38 us  [over_core(): return lax.ppermute(v, 'dp', self.perm_core)]
    unnamed x130 -> x118, local copies, waits for them, and re-layouts: 24.2 us -> 24.1 us
  transfers between devices with their start and end apart: 46 -> 46, of which waited for: 20 -> 23; matrix products, arithmetic and copies ran while one was open for 12% -> 11% of each run, Pallas kernels for 34% -> 34%
where the time goes in v1:
time: 440 us; the launch traced here: 439 us
  waiting for transfers between devices  155 us (35%)
  Pallas kernels  150 us (34%)
  starting transfers between devices  45.5 us (10%)
  local copies, waits for them, and re-layouts  37.9 us (9%)
  other arithmetic  35 us (8%)
  between operations  15 us (3%)
    ppermute x18, waiting for transfers between devices, over_y(): return lax.ppermute(v, 'dp', self.perm_y)  123 us
    pallas_call x12, Pallas kernels, call(): pl.pallas_call(kernel, grid_spec=pltpu.PrefetchScalarGridSpec(num_scalar_...  122 us
    unnamed x118, local copies, waits for them, and re-layouts  24.1 us
    ppermute x18, starting transfers between devices, over_y(): return lax.ppermute(v, 'dp', self.perm_y)  21.6 us
    ppermute x11, waiting for transfers between devices, over_x(): return lax.ppermute(v, 'tensor', [(0, 1), (1, 0)])  16.8 us
    pallas_call x1, Pallas kernels, attend_back(): pl.pallas_call(bwd_kernel, grid_spec=pltpu.PrefetchScalarGridSpec(num_sca...  15.7 us
    ppermute x11, starting transfers between devices, over_x(): return lax.ppermute(v, 'tensor', [(0, 1), (1, 0)])  14.1 us
    pallas_call x1, Pallas kernels, attend(): pl.pallas_call(fwd_kernel, grid_spec=pltpu.PrefetchScalarGridSpec(num_sca...  11.9 us
  transfers between devices with their start and end apart: 46, of which 23 were waited for; matrix products, arithmetic and copies ran while one was open for 11% of the time, Pallas kernels for 34%

profile of v1, /device:TPU:0, one launch (start us, length us, event | category | flops | bytes accessed | tf_op | source)
XLA Modules:
  0.0 439.4 jit_solution(16043246246776255224)
XLA Ops:
  7.3 2.1 constant_dynamic-slice_fusion.14
  9.4 3.0 collective-permute-start.4
  15.1 4.1 collective-permute-start.3
  20.3 5.1 %collective-permute-done.4 = bf16[256,1024]{1,0:T(8,128)(2,1)S(1)} collective-permute-done((bf16[256,1024]{1,0:T(8,128)(2,1)}, bf16[256,1024]{1,0:T(8,128)(2,1)S(1)}, u32[]{:S(2)}, u32[]{:S(2)}) %collective-permute-start.4) | collective-permute-done | bytes 524320 | tf_op jit(solution)/shard_map/ppermute | solution.py:592
  25.3 2.1 collective-permute-start
  28.4 7.4 %collective-permute-done = s32[1,4]{1,0:T(1,128)S(1)} collective-permute-done((s32[1,4]{1,0:T(1,128)S(1)}, s32[1,4]{1,0:T(1,128)S(1)}, u32[]{:S(2)}, u32[]{:S(2)}) %collective-permute-start) | collective-permute-done | bytes 48 | tf_op jit(solution)/shard_map/ppermute | solution.py:592
  35.9 5.5 %collective-permute-done.2 = bf16[128,1024]{1,0:T(8,128)(2,1)} collective-permute-done((bf16[128,1024]{1,0:T(8,128)(2,1)}, bf16[128,1024]{1,0:T(8,128)(2,1)}, u32[]{:S(2)}, u32[]{:S(2)}) %collective-permute-start.2) | collective-permute-done | bytes 262176 | tf_op jit(solution)/shard_map/ppermute | solution.py:601
  50.0 5.8 %norm_rows.2 = (bf16[512,4096]{1,0:T(8,128)(2,1)S(1)}, f32[512,128]{1,0:T(8,128)S(1)}) custom-call(bf16[512,4096]{1,0:T(8,128)(2,1)} %ctx_ref.1, f32[1,4096]{1,0:T(1,128)S(1)} %bitcast.195), custom_call_target="tpu_custom_call" | custom-call | flops 8388608 | bytes 8667136 | tf_op jit(solution)/shard_map/norm_rows/pallas_call | solution.py:232
  55.9 2.1 copy-done.2
  57.9 8.2 %collective-permute-done.6 = bf16[512,1024]{1,0:T(8,128)(2,1)S(1)} collective-permute-done((bf16[512,1024]{1,0:T(8,128)(2,1)S(1)}, bf16[512,1024]{1,0:T(8,128)(2,1)S(1)}, u32[]{:S(2)}, u32[]{:S(2)}) %collective-permute-start.6) | collective-permute-done | bytes 1048608 | tf_op jit(solution)/shard_map/ppermute | solution.py:592
  70.3 42.1 %collective-permute-done.8.refs_1_.refs_6_ = bf16[256,4096]{1,0:T(8,128)(2,1)S(1)} collective-permute-done((bf16[256,4096]{1,0:T(8,128)(2,1)S(1)}, bf16[256,4096]{1,0:T(8,128)(2,1)S(1)}, u32[]{:S(2)}, u32[]{:S(2)}) %collective-permute-start.8) | collective-permute-done | bytes 2097184 | tf_op jit(solution)/shard_map/ppermute | solution.py:592
  113.9 2.1 pad_maximum_fusion.9
  116.0 2.4 collective-permute-done.11.refs_3_
  118.4 5.6 %all-gather.3.cloned.1.call-done.refs_2_.refs_8_ = bf16[4096,1024]{1,0:T(8,128)(2,1)} async-done(((bf16[512,1024]{1,0:T(8,128)(2,1)}), bf16[4096,1024]{1,0:T(8,128)(2,1)}) %all-gather.3.cloned.1.call-update) | async-done | bytes 8388624 | tf_op jit(solution)/shard_map/all_gather | solution.py:673
  127.6 12.2 %rows_times_kv.1 = (bf16[512,1024]{1,0:T(8,128)(2,1)S(1)}, bf16[4096,1024]{1,0:T(8,128)(2,1)}) custom-call(s32[32]{0:T(128)S(1)} %stack.372.offsets_ref, bf16[512,4096]{1,0:T(8,128)(2,1)} %copy-done.2, bf16[1024,1024]{1,0:T(8,128)(2,1)S(1)} %copy-done.29, bf16[1024,1024]{1,0:T(8,128)(2,1)} %collective-permute-done.9.refs_1_, ...), custom_call_target="tpu_custom_call" | custom-call | flops 4294967296 | bytes 22020096 | tf_op jit(solution)/shard_map/rows_times_kv/pallas_call | solution.py:232
  142.7 7.4 %collective-permute-done.12 = bf16[128,4096]{1,0:T(8,128)(2,1)} collective-permute-done((bf16[128,4096]{1,0:T(8,128)(2,1)}, bf16[128,4096]{1,0:T(8,128)(2,1)}, u32[]{:S(2)}, u32[]{:S(2)}) %collective-permute-start.12) | collective-permute-done | bytes 1048608 | tf_op jit(solution)/shard_map/ppermute | solution.py:592
  151.8 4.7 %norm_rows.3 = (bf16[512,4096]{1,0:T(8,128)(2,1)}, f32[512,128]{1,0:T(8,128)S(1)}) custom-call(bf16[256,4096]{1,0:T(8,128)(2,1)S(1)} %copy-done.4, bf16[256,4096]{1,0:T(8,128)(2,1)S(1)} %copy-done.11, f32[1,4096]{1,0:T(1,128)S(1)} %bitcast.194), custom_call_target="tpu_custom_call" | custom-call | flops 8388608 | bytes 8667136 | tf_op jit(solution)/shard_map/norm_rows/pallas_call | solution.py:232
  159.7 3.2 constant_dynamic-slice_fusion.12
  162.9 8.5 %collective-permute-done.14 = bf16[1024,256]{1,0:T(8,128)(2,1)S(1)} collective-permute-done((bf16[1024,256]{1,0:T(8,128)(2,1)S(1)}, bf16[1024,256]{1,0:T(8,128)(2,1)S(1)}, u32[]{:S(2)}, u32[]{:S(2)}) %collective-permute-start.14) | collective-permute-done | bytes 524320 | tf_op jit(solution)/shard_map/ppermute | solution.py:592
  174.3 8.8 %rows_times_weight.2.q_ref = bf16[512,1024]{1,0:T(8,128)(2,1)S(1)} custom-call(s32[16]{0:T(128)S(1)} %stack.335.refs_0_, bf16[512,4096]{1,0:T(8,128)(2,1)S(1)} %copy-done.3, bf16[4096,1024]{1,0:T(8,128)(2,1)} %all-gather.3.cloned.1.call-done.refs_2_.refs_8_), custom_call_target="tpu_custom_call" | custom-call | flops 4294967296 | bytes 13631488 | tf_op jit(solution)/shard_map/rows_times_weight/pallas_call | solution.py:232
  183.2 11.9 %attention_forward.1 = (bf16[512,1024]{1,0:T(8,128)(2,1)S(1)}, f32[8,1,512]{2,1,0:T(1,128)S(1)}) custom-call(s32[2,8]{1,0:T(2,128)S(1)} %pad_add_fusion.1.bounds, bf16[512,1024]{1,0:T(8,128)(2,1)S(1)} %rows_times_weight.2.q_ref, bf16[2,1024,256]{2,1,0:T(8,128)(2,1)S(1)} %pad_maximum_fusion.8.kvp_ref, bf16[512,256]{1,0:T(8,128)(2,1)S(1)} %convolution_convert_fusion.kvl_ref), custom_call_target="tpu_custom_call" | custom-call | flops 2147483648 | bytes 3145728 | tf_op jit(solution)/shard_map/attention_forward/pallas_call | solution.py:163
  197.5 11.7 %weight_grad.2 = bf16[16,256,1024]{2,1,0:T(8,128)(2,1)} custom-call(s32[16]{0:T(128)S(1)} %stack.397.at, bf16[512,4096]{1,0:T(8,128)(2,1)S(1)} %bitcast.192, bf16[512,1024]{1,0:T(8,128)(2,1)S(1)} %get-tuple-element.94.heads_ref.refs_2_), custom_call_target="tpu_custom_call" | custom-call | flops 4294967296 | bytes 13631488 | tf_op jit(solution)/shard_map/weight_grad/pallas_call | solution.py:232
  209.5 2.2 copy-done.9
  211.6 9.5 %rows_times_weight.3.do_ref = bf16[512,1024]{1,0:T(8,128)(2,1)S(1)} custom-call(s32[16]{0:T(128)S(1)} %stack.335.refs_0_, bf16[512,4096]{1,0:T(8,128)(2,1)S(1)} %bitcast.193, bf16[4096,1024]{1,0:T(8,128)(2,1)} %all-gather.5.cloned.1.call-done.refs_2_.refs_3_), custom_call_target="tpu_custom_call" | custom-call | flops 4294967296 | bytes 13631488 | tf_op jit(solution)/shard_map/rows_times_weight/pallas_call | solution.py:232
  221.2 15.7 %attention_backward.1 = (bf16[512,1024]{1,0:T(8,128)(2,1)S(1)}, bf16[2,1024,256]{2,1,0:T(8,128)(2,1)S(1)}, bf16[512,256]{1,0:T(8,128)(2,1)S(1)}) custom-call(s32[2,8]{1,0:T(2,128)S(1)} %pad_add_fusion.1.bounds, bf16[512,1024]{1,0:T(8,128)(2,1)S(1)} %copy-done.20, bf16[512,1024]{1,0:T(8,128)(2,1)S(1)} %rows_times_weight.3.do_ref, ...), custom_call_target="tpu_custom_call" | custom-call | flops 5368709 | bytes 5242 | tf_op jit(solution)/shard_map/attention_backward/pallas_call | solution.py:195
  240.5 10.1 %heads_times_weight.1 = (bf16[2,128,1536]{2,1,0:T(8,128)(2,1)S(1)}, bf16[2,128,1536]{2,1,0:T(8,128)(2,1)S(1)}, bf16[2,128,2560]{2,1,0:T(8,128)(2,1)S(1)}, bf16[2,128,2560]{2,1,0:T(8,128)(2,1)S(1)}) custom-call(s32[16]{0:T(128)S(1)} %stack.335.refs_0_, s32[2]{0:T(128)S(1)} %pad_add_fusion.2.refs_1_.here, ...), custom_call_target="tpu_custom_call" | custom-call | flops 4294967 | bytes 13631 | tf_op jit(solution)/shard_map/heads_times_weight/pallas_call | solution.py:232
  258.6 14.4 %lat_back.1 = (bf16[2,128,2048]{2,1,0:T(8,128)(2,1)S(1)}, bf16[2,128,2048]{2,1,0:T(8,128)(2,1)S(1)}, bf16[2,128,2048]{2,1,0:T(8,128)(2,1)S(1)}, bf16[2,128,2048]{2,1,0:T(8,128)(2,1)S(1)}, f32[1,4096]{1,0:T(1,128)S(1)}) custom-call(s32[16]{0:T(128)S(1)} %stack.335.refs_0_, s32[2]{0:T(128)S(1)} %pad_add_fusion.2.refs_1_.here, ...), custom_call_target="tpu_custom_call" | custom-call | flops 5368709120 | bytes 20463616 | tf_op jit(solution)/shard_map/lat_back/pallas_call | solution.py:232
  275.0 8.3 %kv_weight_grad.2 = bf16[2,8,128,1024]{3,2,1,0:T(8,128)(2,1)S(1)} custom-call(s32[8]{0:T(128)S(1)} %stack.415.at, s32[2]{0:T(128)S(1)} %pad_add_fusion.2.refs_1_.here, bf16[512,4096]{1,0:T(8,128)(2,1)} %copy-done.2, bf16[512,1024]{1,0:T(8,128)(2,1)S(1)} %pad_maximum_fusion.11.d_kv_ref.d_ref, bf16[512,4096]{1,0:T(8,128)(2,1)} %get-tuple-element.115.refs_1_.lat_ref.act_ref, ...), custom_call_target="tpu_custom_call" | custom-call | flops 2684354560 | bytes 13893632 | tf_op jit(solution)/shard_map/kv_weight_grad/pallas_call | solution.py:232
  283.3 2.0 copy-done.7
  285.2 8.3 %kv_weight_grad.3 = bf16[2,8,128,1024]{3,2,1,0:T(8,128)(2,1)S(1)} custom-call(s32[8]{0:T(128)S(1)} %stack.406.at, s32[2]{0:T(128)S(1)} %pad_add_fusion.2.refs_1_.here, bf16[512,4096]{1,0:T(8,128)(2,1)} %copy-done.2, bf16[512,1024]{1,0:T(8,128)(2,1)S(1)} %pad_maximum_fusion.11.d_kv_ref.d_ref, bf16[512,4096]{1,0:T(8,128)(2,1)} %get-tuple-element.115.refs_1_.lat_ref.act_ref, ...), custom_call_target="tpu_custom_call" | custom-call | flops 2684354560 | bytes 13893632 | tf_op jit(solution)/shard_map/kv_weight_grad/pallas_call | solution.py:232
  295.8 10.1 %weight_grad.3 = bf16[8,256,2048]{2,1,0:T(8,128)(2,1)} custom-call(s32[8]{0:T(128)S(1)} %stack.416.at, bf16[512,4096]{1,0:T(8,128)(2,1)} %get-tuple-element.115.refs_1_.lat_ref.act_ref, bf16[512,2048]{1,0:T(8,128)(2,1)S(1)} %pad_maximum_fusion.4.heads_ref), custom_call_target="tpu_custom_call" | custom-call | flops 4294967296 | bytes 14680064 | tf_op jit(solution)/shard_map/weight_grad/pallas_call | solution.py:232
  306.1 2.0 split.6
  308.9 13.7 %collective-permute-done.24 = bf16[256,1024]{1,0:T(8,128)(2,1)} collective-permute-done((bf16[256,1024]{1,0:T(8,128)(2,1)}, bf16[256,1024]{1,0:T(8,128)(2,1)}, u32[]{:S(2)}, u32[]{:S(2)}) %collective-permute-start.24) | collective-permute-done | bytes 524320 | tf_op jit(solution)/shard_map/ppermute | solution.py:592
  327.0 1.8 fusion.10
  328.8 2.8 fusion.9
  336.9 18.4 %ctx_back.1 = (f32[512,4096]{1,0:T(8,128)}, f32[1,4096]{1,0:T(1,128)S(1)}) custom-call(bf16[512,1024]{1,0:T(8,128)(2,1)S(1)} %pad_maximum_fusion.11.d_kv_ref.d_ref, bf16[4096,1024]{1,0:T(8,128)(2,1)} %get-tuple-element.85.kv_ref, bf16[512,4096]{1,0:T(8,128)(2,1)S(1)} %copy-done.6, f32[512,128]{1,0:T(8,128)S(1)} %copy-done.36, f32[1,4096]{1,0:T(1,128)S(1)} %bitcast.196), custom_call_target="tpu_custom_call" | custom-call | flops 4294967296 | bytes 22315008 | tf_op jit(solution)/shard_map/ctx_back/pallas_call | solution.py:232
  355.4 3.5 collective-permute-done.25
  358.9 6.0 %collective-permute-done.26 = bf16[2,4,128,512]{3,2,1,0:T(8,128)(2,1)} collective-permute-done((bf16[2,4,128,512]{3,2,1,0:T(8,128)(2,1)S(1)}, bf16[2,4,128,512]{3,2,1,0:T(8,128)(2,1)}, u32[]{:S(2)}, u32[]{:S(2)}) %collective-permute-start.26) | collective-permute-done | bytes 1048608 | tf_op jit(solution)/shard_map/ppermute | solution.py:595
  365.2 3.9 bitcast_add_fusion
  369.3 1.8 collective-permute-done.22
  380.5 5.5 %collective-permute-done.28 = bf16[4,128,512]{2,1,0:T(8,128)(2,1)S(1)} collective-permute-done((bf16[4,128,512]{2,1,0:T(8,128)(2,1)S(1)}, bf16[4,128,512]{2,1,0:T(8,128)(2,1)S(1)}, u32[]{:S(2)}, u32[]{:S(2)}) %collective-permute-start.28) | collective-permute-done | bytes 524320 | tf_op jit(solution)/shard_map/ppermute | solution.py:595
  388.7 18.2 %collective-permute-done.27 = bf16[2,128,2048]{2,1,0:T(8,128)(2,1)S(1)} collective-permute-done((bf16[2,128,2048]{2,1,0:T(8,128)(2,1)S(1)}, bf16[2,128,2048]{2,1,0:T(8,128)(2,1)S(1)}, u32[]{:S(2)}, u32[]{:S(2)}) %collective-permute-start.27) | collective-permute-done | bytes 1048608 | tf_op jit(solution)/shard_map/ppermute | solution.py:592
  411.9 3.1 collective-permute-done.38
  415.9 4.8 %collective-permute-done.31 = bf16[128,2048]{1,0:T(8,128)(2,1)S(1)} collective-permute-done((bf16[128,2048]{1,0:T(8,128)(2,1)S(1)}, bf16[128,2048]{1,0:T(8,128)(2,1)S(1)}, u32[]{:S(2)}, u32[]{:S(2)}) %collective-permute-start.31) | collective-permute-done | bytes 524320 | tf_op jit(solution)/shard_map/ppermute | solution.py:595
  420.9 3.2 collective-permute-done.32
  425.6 2.5 fusion.6
  428.1 2.8 convert_element_type.254
  430.9 2.0 convert_add_fusion.1
  (261 shorter events, 82.1 us)
Async XLA Ops:
  7.2 116.8 %all-gather.3.cloned.1.call-start = ((), (), s32[]{:S(2)}) async-start(), calls=%async_computation.2 | async-start | bytes 9437184 | tf_op jit(solution)/shard_map/all_gather | solution.py:673
  9.4 15.9 %collective-permute-start.4 = (bf16[256,1024]{1,0:T(8,128)(2,1)}, bf16[256,1024]{1,0:T(8,128)(2,1)S(1)}, u32[]{:S(2)}, u32[]{:S(2)}) collective-permute-start(bf16[256,1024]{1,0:T(8,128)(2,1)} %get-tuple-element.168), channel_id=1, source_target_pairs={{0,4},{2,6},{4,0},{6,2},{8,12},{10,14},{12,8},{14,10},{16,20},{18,... | collective-permute-start | bytes 1572872 | tf_op jit(solution)/shard_map/ppermute | solution.py:592
  13.4 27.9 %collective-permute-start.5 = (bf16[256,1024]{1,0:T(8,128)(2,1)}, bf16[256,1024]{1,0:T(8,128)(2,1)}, u32[]{:S(2)}, u32[]{:S(2)}) collective-permute-start(bf16[256,1024]{1,0:T(8,128)(2,1)} %get-tuple-element.162), channel_id=1, source_target_pairs={{0,4},{2,6},{4,0},{6,2},{8,12},{10,14},{12,8},{14,10},{16,20},{18,... | collective-permute-start | bytes 1572872 | tf_op jit(solution)/shard_map/ppermute | solution.py:592
  15.1 20.7 %collective-permute-start.3 = (bf16[128,1024]{1,0:T(8,128)(2,1)}, bf16[128,1024]{1,0:T(8,128)(2,1)}, u32[]{:S(2)}, u32[]{:S(2)}) collective-permute-start(bf16[128,1024]{1,0:T(8,128)(2,1)} %get-tuple-element.137), channel_id=1, source_target_pairs={{0,24},{2,26},{4,28},{6,30},{8,0},{10,2},{12,4},{14,6},{16,8},{18,... | collective-permute-start | bytes 786440 | tf_op jit(solution)/shard_map/ppermute | solution.py:601
  19.3 22.1 %collective-permute-start.2 = (bf16[128,1024]{1,0:T(8,128)(2,1)}, bf16[128,1024]{1,0:T(8,128)(2,1)}, u32[]{:S(2)}, u32[]{:S(2)}) collective-permute-start(bf16[128,1024]{1,0:T(8,128)(2,1)} %get-tuple-element.137), channel_id=1, source_target_pairs={{0,16},{2,18},{4,20},{6,22},{8,24},{10,26},{12,28},{14,30},{16,0},... | collective-permute-start | bytes 786440 | tf_op jit(solution)/shard_map/ppermute | solution.py:601
  19.3 22.1 %collective-permute-start.1 = (bf16[128,1024]{1,0:T(8,128)(2,1)}, bf16[128,1024]{1,0:T(8,128)(2,1)}, u32[]{:S(2)}, u32[]{:S(2)}) collective-permute-start(bf16[128,1024]{1,0:T(8,128)(2,1)} %get-tuple-element.137), channel_id=1, source_target_pairs={{0,8},{2,10},{4,12},{6,14},{8,16},{10,18},{12,20},{14,22},{16,24},... | collective-permute-start | bytes 786440 | tf_op jit(solution)/shard_map/ppermute | solution.py:601
  25.3 10.5 %collective-permute-start = (s32[1,4]{1,0:T(1,128)S(1)}, s32[1,4]{1,0:T(1,128)S(1)}, u32[]{:S(2)}, u32[]{:S(2)}) collective-permute-start(s32[1,4]{1,0:T(1,128)S(1)} %copy-done.56), channel_id=1, source_target_pairs={{0,4},{2,6},{4,0},{6,2},{8,12},{10,14},{12,8},{14,10},{16,20},{18,... | collective-permute-start | bytes 56 | tf_op jit(solution)/shard_map/ppermute | solution.py:592
  41.4 168.1 %all-gather.5.cloned.1.call-start = ((), (), s32[]{:S(2)}) async-start(), calls=%async_computation.3 | async-start | bytes 9437184 | tf_op jit(solution)/shard_map/all_gather | solution.py:673
  42.7 23.5 %collective-permute-start.6 = (bf16[512,1024]{1,0:T(8,128)(2,1)S(1)}, bf16[512,1024]{1,0:T(8,128)(2,1)S(1)}, u32[]{:S(2)}, u32[]{:S(2)}) collective-permute-start(bf16[512,1024]{1,0:T(8,128)(2,1)S(1)} %pad_maximum_fusion.6), channel_id=1, source_target_pairs={{0,4},{2,6},{4,0},{6,2},{8,12},{10,14},{12,8},{14,10},{16,20},{18,... | collective-permute-start | bytes 3145736 | tf_op jit(solution)/shard_map/ppermute | solution.py:592
  44.3 23.1 %collective-permute-start.7 = (bf16[128,4096]{1,0:T(8,128)(2,1)S(1)}, bf16[128,4096]{1,0:T(8,128)(2,1)S(1)}, u32[]{:S(2)}, u32[]{:S(2)}) collective-permute-start(bf16[128,4096]{1,0:T(8,128)(2,1)S(1)} %copy-done.43), channel_id=1, source_target_pairs={{0,1},{1,0},{2,3},{3,2},{4,5},{5,4},{6,7},{7,6},{8,9},{9,8},{10,11... | collective-permute-start | bytes 3145736 | tf_op jit(solution)/shard_map/ppermute | solution.py:595
  50.0 63.9 %copy-start.46 = (bf16[256,1024]{1,0:T(8,128)(2,1)S(1)}, bf16[256,1024]{1,0:T(8,128)(2,1)}, u32[]{:S(2)}) copy-start(bf16[256,1024]{1,0:T(8,128)(2,1)} %get-tuple-element.161) | copy-start | bytes 1572868
  57.9 58.1 %copy-start.35 = (f32[512,128]{1,0:T(8,128)}, f32[512,128]{1,0:T(8,128)S(1)}, u32[]{:S(2)}) copy-start(f32[512,128]{1,0:T(8,128)S(1)} %get-tuple-element.112.scale_ref) | copy-start | bytes 786436
  67.4 44.9 %collective-permute-start.8 = (bf16[256,4096]{1,0:T(8,128)(2,1)S(1)}, bf16[256,4096]{1,0:T(8,128)(2,1)S(1)}, u32[]{:S(2)}, u32[]{:S(2)}) collective-permute-start(bf16[256,4096]{1,0:T(8,128)(2,1)S(1)} %copy-done.4), channel_id=1, source_target_pairs={{0,4},{2,6},{4,0},{6,2},{8,12},{10,14},{12,8},{14,10},{16,20},{18,... | collective-permute-start | bytes 6291464 | tf_op jit(solution)/shard_map/ppermute | solution.py:592
  68.8 45.1 %collective-permute-start.9 = (bf16[1024,1024]{1,0:T(8,128)(2,1)}, bf16[1024,1024]{1,0:T(8,128)(2,1)}, u32[]{:S(2)}, u32[]{:S(2)}) collective-permute-start(bf16[1024,1024]{1,0:T(8,128)(2,1)} %constant_dynamic-update-slice_fusion.refs_0_), channel_id=1, source_target_pairs={{0,1},{1,0},{2,3},{3,2},{4,5},{5,4},{6,7},{7,6},{8,9},{9,8},{10,11... | collective-permute-start | bytes 6291464 | tf_op jit(solution)/shard_map/ppermute | solution.py:595
  70.3 45.7 %collective-permute-start.10 = (bf16[1024,1024]{1,0:T(8,128)(2,1)}, bf16[1024,1024]{1,0:T(8,128)(2,1)}, u32[]{:S(2)}, u32[]{:S(2)}) collective-permute-start(bf16[1024,1024]{1,0:T(8,128)(2,1)} %constant_dynamic-update-slice_fusion.refs_0_), channel_id=1, source_target_pairs={{0,2},{2,0},{4,6},{6,4},{8,10},{10,8},{12,14},{14,12},{16,18},{18,... | collective-permute-start | bytes 6291464 | tf_op jit(solution)/shard_map/ppermute | solution.py:589
  113.9 4.5 %collective-permute-start.11 = (bf16[1024,1024]{1,0:T(8,128)(2,1)}, bf16[1024,1024]{1,0:T(8,128)(2,1)}, u32[]{:S(2)}, u32[]{:S(2)}) collective-permute-start(bf16[1024,1024]{1,0:T(8,128)(2,1)} %collective-permute-done.9.refs_1_), channel_id=1, source_target_pairs={{0,2},{2,0},{4,6},{6,4},{8,10},{10,8},{12,14},{14,12},{16,18},{18,... | collective-permute-start | bytes 6291464 | tf_op jit(solution)/shard_map/ppermute | solution.py:589
  124.0 182.0 %reduce-scatter.3.cloned.1.call-start = ((), (), s32[]{:S(2)}) async-start(), calls=%async_computation.4 | async-start | bytes 9437184 | tf_op jit(solution)/shard_map/reduce_scatter | solution.py:747
  124.4 25.7 %collective-permute-start.12 = (bf16[128,4096]{1,0:T(8,128)(2,1)}, bf16[128,4096]{1,0:T(8,128)(2,1)}, u32[]{:S(2)}, u32[]{:S(2)}) collective-permute-start(bf16[128,4096]{1,0:T(8,128)(2,1)} %copy-done.51), channel_id=1, source_target_pairs={{0,4},{2,6},{4,0},{6,2},{8,12},{10,14},{12,8},{14,10},{16,20},{18,... | collective-permute-start | bytes 3145736 | tf_op jit(solution)/shard_map/ppermute | solution.py:592
  140.6 15.8 %collective-permute-start.13 = (bf16[512,512]{1,0:T(8,128)(2,1)}, bf16[512,512]{1,0:T(8,128)(2,1)}, u32[]{:S(2)}, u32[]{:S(2)}) collective-permute-start(bf16[512,512]{1,0:T(8,128)(2,1)} %constant_dynamic-slice_fusion.13), channel_id=1, source_target_pairs={{0,1},{1,0},{2,3},{3,2},{4,5},{5,4},{6,7},{7,6},{8,9},{9,8},{10,11... | collective-permute-start | bytes 1572872 | tf_op jit(solution)/shard_map/ppermute | solution.py:595
  158.1 13.3 %collective-permute-start.14 = (bf16[1024,256]{1,0:T(8,128)(2,1)S(1)}, bf16[1024,256]{1,0:T(8,128)(2,1)S(1)}, u32[]{:S(2)}, u32[]{:S(2)}) collective-permute-start(bf16[1024,256]{1,0:T(8,128)(2,1)S(1)} %pad_maximum_fusion.13), channel_id=1, source_target_pairs={{0,4},{2,6},{4,0},{6,2},{8,12},{10,14},{12,8},{14,10},{16,20},{18,... | collective-permute-start | bytes 1572872 | tf_op jit(solution)/shard_map/ppermute | solution.py:592
  171.4 23.8 %collective-permute-start.15 = (bf16[128,4096]{1,0:T(8,128)(2,1)S(1)}, bf16[128,4096]{1,0:T(8,128)(2,1)S(1)}, u32[]{:S(2)}, u32[]{:S(2)}) collective-permute-start(bf16[128,4096]{1,0:T(8,128)(2,1)S(1)} %copy-done.44), channel_id=1, source_target_pairs={{0,4},{2,6},{4,0},{6,2},{8,12},{10,14},{12,8},{14,10},{16,20},{18,... | collective-permute-start | bytes 3145736 | tf_op jit(solution)/shard_map/ppermute | solution.py:592
  209.2 218.9 %reduce-scatter.5.cloned.1.call-start = ((), (), s32[]{:S(2)}) async-start(), calls=%async_computation.5 | async-start | bytes 9437184 | tf_op jit(solution)/shard_map/reduce_scatter | solution.py:731
  238.7 11.9 %collective-permute-start.16 = (bf16[1024,256]{1,0:T(8,128)(2,1)}, bf16[1024,256]{1,0:T(8,128)(2,1)S(1)}, u32[]{:S(2)}, u32[]{:S(2)}) collective-permute-start(bf16[1024,256]{1,0:T(8,128)(2,1)} %slice_bitcast_fusion.4), channel_id=1, source_target_pairs={{0,4},{2,6},{4,0},{6,2},{8,12},{10,14},{12,8},{14,10},{16,20},{18,... | collective-permute-start | bytes 1572872 | tf_op jit(solution)/shard_map/ppermute | solution.py:592
  252.2 20.9 %collective-permute-start.18 = (bf16[512,512]{1,0:T(8,128)(2,1)S(1)}, bf16[512,512]{1,0:T(8,128)(2,1)S(1)}, u32[]{:S(2)}, u32[]{:S(2)}) collective-permute-start(bf16[512,512]{1,0:T(8,128)(2,1)S(1)} %dynamic-slice_bitcast_fusion), channel_id=1, source_target_pairs={{0,1},{1,0},{2,3},{3,2},{4,5},{5,4},{6,7},{7,6},{8,9},{9,8},{10,11... | collective-permute-start | bytes 1572872 | tf_op jit(solution)/shard_map/ppermute | solution.py:595
  255.3 40.5 %collective-permute-start.17 = (bf16[2,128,1536]{2,1,0:T(8,128)(2,1)S(1)}, bf16[2,128,1536]{2,1,0:T(8,128)(2,1)S(1)}, u32[]{:S(2)}, u32[]{:S(2)}) collective-permute-start(bf16[2,128,1536]{2,1,0:T(8,128)(2,1)S(1)} %get-tuple-element.98), channel_id=1, source_target_pairs={{0,4},{2,6},{4,0},{6,2},{8,12},{10,14},{12,8},{14,10},{16,20},{18,... | collective-permute-start | bytes 2359304 | tf_op jit(solution)/shard_map/ppermute | solution.py:592
  255.9 37.7 %collective-permute-start.23 = (bf16[512,1024]{1,0:T(8,128)(2,1)S(1)}, bf16[512,1024]{1,0:T(8,128)(2,1)S(1)}, u32[]{:S(2)}, u32[]{:S(2)}) collective-permute-start(bf16[512,1024]{1,0:T(8,128)(2,1)S(1)} %get-tuple-element.116.refs_2_), channel_id=1, source_target_pairs={{0,4},{2,6},{4,0},{6,2},{8,12},{10,14},{12,8},{14,10},{16,20},{18,... | collective-permute-start | bytes 3145736 | tf_op jit(solution)/shard_map/ppermute | solution.py:592
  257.3 38.5 %collective-permute-start.21 = (bf16[2,128,2560]{2,1,0:T(8,128)(2,1)S(1)}, bf16[2,128,2560]{2,1,0:T(8,128)(2,1)S(1)}, u32[]{:S(2)}, u32[]{:S(2)}) collective-permute-start(bf16[2,128,2560]{2,1,0:T(8,128)(2,1)S(1)} %get-tuple-element.109), channel_id=1, source_target_pairs={{0,1},{1,0},{2,3},{3,2},{4,5},{5,4},{6,7},{7,6},{8,9},{9,8},{10,11... | collective-permute-start | bytes 3932168 | tf_op jit(solution)/shard_map/ppermute | solution.py:595
  306.0 19.6 %collective-permute-start.19 = (bf16[2,2,4,128,1024]{4,3,2,1,0:T(8,128)(2,1)}, bf16[2,2,4,128,1024]{4,3,2,1,0:T(8,128)(2,1)}, u32[]{:S(2)}, u32[]{:S(2)}) collective-permute-start(bf16[2,2,4,128,1024]{4,3,2,1,0:T(8,128)(2,1)} %bitcast.191), channel_id=1, source_target_pairs={{0,2},{2,0},{4,6},{6,4},{8,10},{10,8},{12,14},{14,12},{16,18},{18,... | collective-permute-start | bytes 12582920 | tf_op jit(solution)/shard_map/ppermute | solution.py:589
  308.1 14.5 %collective-permute-start.24 = (bf16[256,1024]{1,0:T(8,128)(2,1)}, bf16[256,1024]{1,0:T(8,128)(2,1)}, u32[]{:S(2)}, u32[]{:S(2)}) collective-permute-start(bf16[256,1024]{1,0:T(8,128)(2,1)} %split.6), channel_id=1, source_target_pairs={{0,4},{2,6},{4,0},{6,2},{8,12},{10,14},{12,8},{14,10},{16,20},{18,... | collective-permute-start | bytes 1572872 | tf_op jit(solution)/shard_map/ppermute | solution.py:592
  331.7 23.6 %collective-permute-start.20 = (bf16[128,1536]{1,0:T(8,128)(2,1)S(1)}, bf16[128,1536]{1,0:T(8,128)(2,1)S(1)}, u32[]{:S(2)}, u32[]{:S(2)}) collective-permute-start(bf16[128,1536]{1,0:T(8,128)(2,1)S(1)} %fusion.20), channel_id=1, source_target_pairs={{0,1},{1,0},{2,3},{3,2},{4,5},{5,4},{6,7},{7,6},{8,9},{9,8},{10,11... | collective-permute-start | bytes 1179656 | tf_op jit(solution)/shard_map/ppermute | solution.py:595
  332.5 26.4 %collective-permute-start.25 = (bf16[2,4,128,512]{3,2,1,0:T(8,128)(2,1)}, bf16[2,4,128,512]{3,2,1,0:T(8,128)(2,1)}, u32[]{:S(2)}, u32[]{:S(2)}) collective-permute-start(bf16[2,4,128,512]{3,2,1,0:T(8,128)(2,1)} %fusion.9), channel_id=1, source_target_pairs={{0,4},{2,6},{4,0},{6,2},{8,12},{10,14},{12,8},{14,10},{16,20},{18,... | collective-permute-start | bytes 3145736 | tf_op jit(solution)/shard_map/ppermute | solution.py:592
  333.1 31.9 %collective-permute-start.26 = (bf16[2,4,128,512]{3,2,1,0:T(8,128)(2,1)S(1)}, bf16[2,4,128,512]{3,2,1,0:T(8,128)(2,1)}, u32[]{:S(2)}, u32[]{:S(2)}) collective-permute-start(bf16[2,4,128,512]{3,2,1,0:T(8,128)(2,1)S(1)} %fusion.10), channel_id=1, source_target_pairs={{0,1},{1,0},{2,3},{3,2},{4,5},{5,4},{6,7},{7,6},{8,9},{9,8},{10,11... | collective-permute-start | bytes 3145736 | tf_op jit(solution)/shard_map/ppermute | solution.py:595
  335.4 35.7 %collective-permute-start.22 = (bf16[128,2560]{1,0:T(8,128)(2,1)}, bf16[128,2560]{1,0:T(8,128)(2,1)}, u32[]{:S(2)}, u32[]{:S(2)}) collective-permute-start(bf16[128,2560]{1,0:T(8,128)(2,1)} %fusion.13), channel_id=1, source_target_pairs={{0,4},{2,6},{4,0},{6,2},{8,12},{10,14},{12,8},{14,10},{16,20},{18,... | collective-permute-start | bytes 1966088 | tf_op jit(solution)/shard_map/ppermute | solution.py:592
  365.1 8.0 %collective-permute-start.33 = (f32[2,4,2,2,128]{4,3,2,0,1:T(2,128)S(1)}, f32[2,4,2,2,128]{4,3,2,0,1:T(2,128)S(1)}, u32[]{:S(2)}, u32[]{:S(2)}) collective-permute-start(f32[2,4,2,2,128]{4,3,2,0,1:T(2,128)S(1)} %bitcast.206), channel_id=1, source_target_pairs={{0,2},{2,0},{4,6},{6,4},{8,10},{10,8},{12,14},{14,12},{16,18},{18,... | collective-permute-start | bytes 49160 | tf_op jit(solution)/shard_map/ppermute | solution.py:589
  371.1 14.9 %collective-permute-start.28 = (bf16[4,128,512]{2,1,0:T(8,128)(2,1)S(1)}, bf16[4,128,512]{2,1,0:T(8,128)(2,1)S(1)}, u32[]{:S(2)}, u32[]{:S(2)}) collective-permute-start(bf16[4,128,512]{2,1,0:T(8,128)(2,1)S(1)} %fusion.16), channel_id=1, source_target_pairs={{0,1},{1,0},{2,3},{3,2},{4,5},{5,4},{6,7},{7,6},{8,9},{9,8},{10,11... | collective-permute-start | bytes 1572872 | tf_op jit(solution)/shard_map/ppermute | solution.py:595
  372.5 14.9 %collective-permute-start.29 = (bf16[4,128,512]{2,1,0:T(8,128)(2,1)S(1)}, bf16[4,128,512]{2,1,0:T(8,128)(2,1)S(1)}, u32[]{:S(2)}, u32[]{:S(2)}) collective-permute-start(bf16[4,128,512]{2,1,0:T(8,128)(2,1)S(1)} %fusion.17), channel_id=1, source_target_pairs={{0,4},{2,6},{4,0},{6,2},{8,12},{10,14},{12,8},{14,10},{16,20},{18,... | collective-permute-start | bytes 1572872 | tf_op jit(solution)/shard_map/ppermute | solution.py:592
  373.1 4.0 collective-permute-start.34
  373.7 5.7 %collective-permute-start.36 = (f32[2,2,2,128]{3,2,1,0:T(2,128)S(1)}, f32[2,2,2,128]{3,2,1,0:T(2,128)S(1)}, u32[]{:S(2)}, u32[]{:S(2)}) collective-permute-start(f32[2,2,2,128]{3,2,1,0:T(2,128)S(1)} %get-tuple-element.176), channel_id=1, source_target_pairs={{0,8},{2,10},{4,12},{6,14},{8,16},{10,18},{12,20},{14,22},{16,24},... | collective-permute-start | bytes 12296 | tf_op jit(solution)/shard_map/ppermute | solution.py:601
  375.2 5.3 %collective-permute-start.35 = (f32[2,2,2,128]{3,2,1,0:T(2,128)S(1)}, f32[2,2,2,128]{3,2,1,0:T(2,128)S(1)}, u32[]{:S(2)}, u32[]{:S(2)}) collective-permute-start(f32[2,2,2,128]{3,2,1,0:T(2,128)S(1)} %get-tuple-element.177), channel_id=1, source_target_pairs={{0,16},{2,18},{4,20},{6,22},{8,24},{10,26},{12,28},{14,30},{16,0},... | collective-permute-start | bytes 12296 | tf_op jit(solution)/shard_map/ppermute | solution.py:601
  377.0 29.9 %collective-permute-start.27 = (bf16[2,128,2048]{2,1,0:T(8,128)(2,1)S(1)}, bf16[2,128,2048]{2,1,0:T(8,128)(2,1)S(1)}, u32[]{:S(2)}, u32[]{:S(2)}) collective-permute-start(bf16[2,128,2048]{2,1,0:T(8,128)(2,1)S(1)} %copy-done.34), channel_id=1, source_target_pairs={{0,4},{2,6},{4,0},{6,2},{8,12},{10,14},{12,8},{14,10},{16,20},{18,... | collective-permute-start | bytes 3145736 | tf_op jit(solution)/shard_map/ppermute | solution.py:592
  379.4 27.5 %collective-permute-start.30 = (bf16[2,128,2048]{2,1,0:T(8,128)(2,1)S(1)}, bf16[2,128,2048]{2,1,0:T(8,128)(2,1)S(1)}, u32[]{:S(2)}, u32[]{:S(2)}) collective-permute-start(bf16[2,128,2048]{2,1,0:T(8,128)(2,1)S(1)} %copy-done.32), channel_id=1, source_target_pairs={{0,1},{1,0},{2,3},{3,2},{4,5},{5,4},{6,7},{7,6},{8,9},{9,8},{10,11... | collective-permute-start | bytes 3145736 | tf_op jit(solution)/shard_map/ppermute | solution.py:595
  406.9 4.3 collective-permute-start.37
  408.1 22.8 %collective-permute-start.39 = (bf16[128,1024]{1,0:T(8,128)(2,1)}, bf16[128,1024]{1,0:T(8,128)(2,1)}, u32[]{:S(2)}, u32[]{:S(2)}) collective-permute-start(bf16[128,1024]{1,0:T(8,128)(2,1)} %get-tuple-element.133), channel_id=1, source_target_pairs={{0,24},{2,26},{4,28},{6,30},{8,0},{10,2},{12,4},{14,6},{16,8},{18,... | collective-permute-start | bytes 786440 | tf_op jit(solution)/shard_map/ppermute | solution.py:601
  409.1 21.8 %collective-permute-start.40 = (bf16[128,1024]{1,0:T(8,128)(2,1)}, bf16[128,1024]{1,0:T(8,128)(2,1)}, u32[]{:S(2)}, u32[]{:S(2)}) collective-permute-start(bf16[128,1024]{1,0:T(8,128)(2,1)} %get-tuple-element.134), channel_id=1, source_target_pairs={{0,16},{2,18},{4,20},{6,22},{8,24},{10,26},{12,28},{14,30},{16,0},... | collective-permute-start | bytes 786440 | tf_op jit(solution)/shard_map/ppermute | solution.py:601
  409.1 21.8 %collective-permute-start.41 = (bf16[128,1024]{1,0:T(8,128)(2,1)}, bf16[128,1024]{1,0:T(8,128)(2,1)}, u32[]{:S(2)}, u32[]{:S(2)}) collective-permute-start(bf16[128,1024]{1,0:T(8,128)(2,1)} %get-tuple-element.135), channel_id=1, source_target_pairs={{0,8},{2,10},{4,12},{6,14},{8,16},{10,18},{12,20},{14,22},{16,24},... | collective-permute-start | bytes 786440 | tf_op jit(solution)/shard_map/ppermute | solution.py:601
  410.2 10.5 %collective-permute-start.31 = (bf16[128,2048]{1,0:T(8,128)(2,1)S(1)}, bf16[128,2048]{1,0:T(8,128)(2,1)S(1)}, u32[]{:S(2)}, u32[]{:S(2)}) collective-permute-start(bf16[128,2048]{1,0:T(8,128)(2,1)S(1)} %fusion.14), channel_id=1, source_target_pairs={{0,1},{1,0},{2,3},{3,2},{4,5},{5,4},{6,7},{7,6},{8,9},{9,8},{10,11... | collective-permute-start | bytes 1572872 | tf_op jit(solution)/shard_map/ppermute | solution.py:595
  411.2 3.7 collective-permute-start.38
  414.9 9.2 %collective-permute-start.32 = (bf16[128,2048]{1,0:T(8,128)(2,1)S(1)}, bf16[128,2048]{1,0:T(8,128)(2,1)S(1)}, u32[]{:S(2)}, u32[]{:S(2)}) collective-permute-start(bf16[128,2048]{1,0:T(8,128)(2,1)S(1)} %fusion.15), channel_id=1, source_target_pairs={{0,4},{2,6},{4,0},{6,2},{8,12},{10,14},{12,8},{14,10},{16,20},{18,... | collective-permute-start | bytes 1572872 | tf_op jit(solution)/shard_map/ppermute | solution.py:592
  (55 other events, 447.4 us)
Sparse Core Ops, SparseCore 0:
  41.5 82.4 all-gather.2
  125.6 80.5 all-gather.4
  209.3 87.9 reduce-scatter.2
  306.1 86.9 reduce-scatter.4
